TPU v7x, 32 devices: a whole 2x2x4 slice. The times are simulated.
32 devices in a mesh: seq: 32 (over z, y, x, core), dp: 1.
Axes of the slice: x: 2, y: 2, z: 4, core: 2. Of those that a mesh axis runs over, the one named last changes fastest.
Arguments:
- queries: bfloat16 [4096, 1024], P(('dp', 'seq')), may hold values from -6 to 6
- keys: bfloat16 [4096, 1024], P(('dp', 'seq')), may hold values from -4 to 4
- values: bfloat16 [4096, 1024], P(('dp', 'seq')), may hold values from -6 to 6
- cotangent: bfloat16 [4096, 1024], P(('dp', 'seq')), may hold values from -6 to 6
- doc_ids: int32 [4096], P(('dp', 'seq')), may hold values from 0 to 7, never falling along the last dimension, each value on 1 to 2048 neighbouring positions
Outputs:
- attended: bfloat16 [4096, 1024], P(('dp', 'seq'))
- grad_queries: bfloat16 [4096, 1024], P(('dp', 'seq'))
- grad_keys: bfloat16 [4096, 1024], P(('dp', 'seq'))
- grad_values: bfloat16 [4096, 1024], P(('dp', 'seq'))
Inputs may be any that keep to these rules, and one draw needn't show every extreme that they name: doc_ids never fall along the sequence; each document holds 1 to 2048 positions.
All inputs are finite; a program needn't handle non-finite values.
Results may differ from a plain program's by a relative error of at most 0.0058.
Values may be sent and summed in bfloat16 or wider, within the bound.
No kernel may reach another device: no remote copies, remote signals or barrier semaphores. Data moves between devices by JAX's collectives and lax.ppermute only.
A program may use at most 128 MiB of HBM per device.

v0:
```python
import functools

import jax
import jax.numpy as jnp
import numpy as np
from jax import lax
from jax.experimental import pallas as pl
from jax.experimental.pallas import tpu as pltpu
from jax.sharding import Mesh
from jax.sharding import PartitionSpec as P

H = 8
HD = 128
SEG = 1024

MASKED = -1e30
SCALE = HD ** -0.5
LOG2E = float(np.log2(np.e))
VMEM = pl.BlockSpec(memory_space=pltpu.VMEM)
DOC_ROWS = 16


def dot_nn(a, b):
    return lax.dot_general(a, b, (((1,), (0,)), ((), ())), preferred_element_type=jnp.float32)


def dot_nt(a, b):
    return lax.dot_general(a, b, (((1,), (1,)), ((), ())), preferred_element_type=jnp.float32)


def selector(head, r0, rows, tokens, transposed, fine_first=False):
    r1 = 2 * r0
    shape = (tokens, 2 * rows) if transposed else (2 * rows, tokens)
    k = lax.broadcasted_iota(jnp.int32, shape, 1 if transposed else 0)
    p = lax.broadcasted_iota(jnp.int32, shape, 0 if transposed else 1)
    coarse = head % r1
    other = (coarse + r0) % r1
    first, second = jnp.where(fine_first, other, coarse), jnp.where(fine_first, coarse, other)
    target = jnp.where(k < rows, r1 * k + first, r1 * (k - rows) + second)
    return (p == target).astype(jnp.float32).astype(jnp.bfloat16)


def takes_fine(members):
    return lax.axis_index("member") >= members // 2


def pack_kernel(r0, rows, members, q_in, k_in, v_in, g_in, doc_in, out, q_ref, k_ref, v_ref, g_ref, doc_ref, buf, sem):
    tokens = q_ref.shape[0]
    pairs = ((doc_in, doc_ref), (k_in, k_ref), (v_in, v_ref), (q_in, q_ref), (g_in, g_ref))
    copies = [pltpu.make_async_copy(src, dst, sem.at[i]) for i, (src, dst) in enumerate(pairs)]
    for copy in copies:
        copy.start()
    kinds = range(min(H, 2 * r0))
    key_sels = [selector(h, r0, rows, tokens, False) for h in kinds]
    query_sels = [selector(h, r0, rows, tokens, False, takes_fine(members)) for h in kinds]

    def pick(sels, h, ref):
        return dot_nn(sels[h % (2 * r0)], ref[:, h * HD:(h + 1) * HD]).astype(jnp.bfloat16)

    for copy in copies:
        copy.wait()
    docs = jnp.broadcast_to(doc_ref[...].astype(jnp.float32).astype(jnp.bfloat16), (DOC_ROWS, tokens))
    sends = []
    for h in range(H):
        for i, ref in enumerate((q_ref, g_ref)):
            x = pick(query_sels, h, ref)
            buf[h, i * rows:(1 + i) * rows] = x[:rows]
            buf[h, (2 + i) * rows:(3 + i) * rows] = x[rows:]
        for i, ref in enumerate((k_ref, v_ref)):
            x = pick(key_sels, h, ref)
            buf[h, (4 + i) * rows:(5 + i) * rows] = x[rows:]
            buf[h, (6 + i) * rows:(7 + i) * rows] = x[:rows]
        buf[h, 8 * rows:8 * rows + DOC_ROWS] = docs
        sends.append(pltpu.make_async_copy(buf.at[h], out.at[h], sem.at[5 + h]))
        sends[-1].start()
    for copy in sends:
        copy.wait()


TILES = 2


def tile_sizes(rows, members):
    per = H // TILES
    return per * members * rows, per * 2 * rows


def eye_matrix():
    shape = (HD, HD)
    same = lax.broadcasted_iota(jnp.int32, shape, 0) == lax.broadcasted_iota(jnp.int32, shape, 1)
    return same.astype(jnp.float32).astype(jnp.bfloat16)


def doc_cols(x):
    return dot_nn(x, jnp.ones((HD, HD), jnp.bfloat16))[:, 0:1]


def local_kernel(r0, rows, members, *refs):
    G = members
    r1 = 2 * r0
    own_ref, swap_refs = refs[0], refs[1:G]
    (k1, k2, q_all, g_all, stats, out_ref, gtt_ref), rest = refs[G:G + 7], refs[G + 7:]
    p_refs, dp_refs, (v1, v2, d1, d2) = rest[:2 * TILES], rest[2 * TILES:4 * TILES], rest[4 * TILES:]
    bf16, f32 = jnp.bfloat16, jnp.float32
    tokens = HD
    head = lax.axis_index("head")
    member = lax.axis_index("member")
    fine = takes_fine(G)
    partner = G // 2
    partner_ref = swap_refs[partner - 1]

    sel = selector(head, r0, rows, tokens, False)
    query_sel = jnp.where(fine, sel[rows:].astype(f32), sel[:rows].astype(f32)).astype(bf16)
    source_docs = []
    for j in range(H):
        for g in range(G):
            at = pl.ds((j * G + g) * rows, rows)
            ref, base = (own_ref, 4 * rows) if g == 0 else (swap_refs[g - 1], 2 * rows if g == partner else 0)
            k2[at] = ref[j, base:base + rows]
            v2[at] = ref[j, base + rows:base + 2 * rows]
            k1[at] = ref[j, base + 2 * rows:base + 3 * rows]
            v1[at] = ref[j, base + 3 * rows:base + 4 * rows]
            doc = ref[j, base + 4 * rows:base + 4 * rows + DOC_ROWS][0:1]
            if g in (0, partner):
                source_docs.append(doc)
            d1[at] = sel[:rows] * doc
            d2[at] = sel[rows:] * doc

    eye = eye_matrix()
    v1t, v2t = dot_nt(eye, v1[...]).astype(bf16), dot_nt(eye, v2[...]).astype(bf16)
    docs1, docs2 = doc_cols(d1[...]), doc_cols(d2[...])
    nd, lanes = tile_sizes(rows, G)
    per = H // TILES

    coarse = head % r1
    other = (coarse + r0) % r1
    lane = lax.broadcasted_iota(jnp.int32, (1, lanes), 1)
    qmember = member ^ (partner * ((lane // rows) % 2))
    qpos = (lane // (2 * rows)) * (G * tokens) + qmember * tokens + r1 * (lane % rows) + jnp.where(fine, other, coarse)
    kl = lax.broadcasted_iota(jnp.int32, (nd, 1), 0)
    kmember = member ^ ((kl // rows) % G)
    kpos = (kl // (rows * G)) * (G * tokens) + kmember * tokens + r1 * (kl % rows)
    causal1 = kpos + coarse <= qpos
    causal2 = kpos + other <= qpos
    both = jnp.where(fine, 0.0, 1.0)
    c = SCALE * LOG2E

    for u in range(TILES):
        nk = (u + 1) * nd
        x0 = u * nd
        src = range(u * per, (u + 1) * per)
        mine = slice(u * lanes, (u + 1) * lanes)
        gather = lambda lo: jnp.concatenate([ref[j, lo:lo + rows] for j in src for ref in (own_ref, partner_ref)], 0)
        qt, gt = gather(0), gather(rows)
        q_all[mine], g_all[mine] = qt, gt
        dq = jnp.concatenate([query_sel * source_docs[2 * j + e] for j in src for e in range(2)], 0)
        qdoc = dot_nt(jnp.ones((16, HD), bf16), dq)[0:1]

        def scores(key, docs, causal):
            s = jnp.where(docs == qdoc, dot_nt(key, qt), MASKED)
            if u:
                return jnp.concatenate([s[:x0], jnp.where(causal, s[x0:], MASKED)], 0)
            return jnp.where(causal, s, MASKED)

        s1 = scores(k1[0:nk], docs1[0:nk], causal1)
        s2 = scores(k2[0:nk], docs2[0:nk], causal2)
        top = jnp.maximum(jnp.max(s1, 0, keepdims=True), jnp.max(s2, 0, keepdims=True))
        base = top * c
        p1 = jnp.exp2(s1 * c - (base - both))
        p2 = jnp.exp2(s2 * c - base)
        stats[0:1, mine] = top
        stats[1:2, mine] = jnp.sum(p1, 0, keepdims=True) + jnp.sum(p2, 0, keepdims=True)
        stats[2:3, mine] = qdoc
        out_ref[:, mine] = dot_nn(v1t[:, :nk], p1.astype(bf16)) + dot_nn(v2t[:, :nk], p2.astype(bf16))
        gtt_ref[:, mine] = dot_nt(eye, gt)
        p_refs[2 * u][...], p_refs[2 * u + 1][...] = p1, p2
        dp_refs[2 * u][...], dp_refs[2 * u + 1][...] = dot_nt(v1[0:nk], gt), dot_nt(v2[0:nk], gt)


def finish_tile(u, r0, rows, members, parts, shared, products, results, scratch):
    far = (lax.axis_index("half") == 1) & jnp.logical_not(takes_fine(members))
    for branch, with_far in ((far, True), (jnp.logical_not(far), False)):
        pl.when(branch)(functools.partial(
            tile_body, u, r0, rows, members, with_far, parts, shared, products, results, scratch))


def tile_body(u, r0, rows, members, with_far, parts, shared, products, results, scratch):
    G = members
    q_all, g_all, stats, local_out, gtt_ref, k1, k2 = shared
    far_stats, att, gq_ref, sums = results[0], results[1], results[2], results[3:]
    kx, vx, dx = scratch
    bf16 = jnp.bfloat16
    per = H // TILES
    eye = eye_matrix()
    nd, lanes = tile_sizes(rows, G)
    nk = (u + 1) * nd
    mine = slice(u * lanes, (u + 1) * lanes)
    c = SCALE * LOG2E
    qt, gt = q_all[mine], g_all[mine]
    top, total, out = stats[0:1, mine], stats[1:2, mine], local_out[:, mine]
    if with_far:
        sel = selector(lax.axis_index("head"), r0, rows, HD, False)
        for p, part in enumerate(parts):
            for j in range(per):
                for g, ref in enumerate(part):
                    at = pl.ds(((p * per + j) * G + g) * rows, rows)
                    kx[at] = ref[2 * j * rows:(2 * j + 1) * rows]
                    vx[at] = ref[(2 * j + 1) * rows:(2 * j + 2) * rows]
                    dx[at] = sel[:rows] * ref[2 * per * rows:2 * per * rows + DOC_ROWS][j:j + 1]
        keys_x, values_x = kx[...], vx[...]
        kxt, vxt = dot_nt(eye, keys_x).astype(bf16), dot_nt(eye, values_x).astype(bf16)
        sx = jnp.where(doc_cols(dx[...]) == stats[2:3, mine], dot_nt(keys_x, qt), MASKED)
        local_top = top
        top = jnp.maximum(local_top, jnp.max(sx, 0, keepdims=True))
        px = jnp.exp2(sx * c - top * c)
        shrink = jnp.exp2(local_top * c - top * c)
        total = total * shrink + jnp.sum(px, 0, keepdims=True)
        inv = 1.0 / total
        local_inv = shrink * inv
        out = out * local_inv + dot_nn(vxt, px.astype(bf16)) * inv
    else:
        local_inv = 1.0 / total
        out = out * local_inv
    dot = jnp.sum(gtt_ref[:, mine] * out, 0, keepdims=True)
    lse = top * c + jnp.log(total) * LOG2E
    chunks = lanes // HD
    for i in range(chunks):
        far_stats[u * chunks + i:u * chunks + i + 1] = lse[:, i * HD:(i + 1) * HD]
        far_stats[4 + u * chunks + i:5 + u * chunks + i] = dot[:, i * HD:(i + 1) * HD]
    att[...] = out.T.astype(bf16)
    gq = 0.0
    if with_far:
        ds = (px * inv * (dot_nt(values_x, gt) - dot)).astype(bf16)
        gq = dot_nn(kxt, ds)
    for i, k in enumerate((k1, k2)):
        w = products[i][...] * local_inv
        ds = (w * (products[2 + i][...] - dot)).astype(bf16)
        gq = gq + dot_nn(dot_nt(eye, k[0:nk]).astype(bf16), ds)
        sums[i][...] = dot_nn(ds, qt)
        sums[2 + i][...] = dot_nn(w.astype(bf16), gt)
    gq_ref[...] = (gq * SCALE).T.astype(bf16)


def last_tile_kernel(r0, rows, members, *refs):
    G = members
    finish_tile(1, r0, rows, G, [refs[:G]], refs[G:G + 7], refs[G + 7:G + 11], refs[G + 11:G + 18], refs[G + 18:])


def first_tile_kernel(r0, rows, members, *refs):
    G = members
    parts, refs = [refs[:G], refs[G:2 * G]], refs[2 * G:]
    shared, products, last, refs = refs[:7], refs[7:11], refs[11:18], refs[18:]
    far_stats, out_own, out_kv, out_swap, scratch = refs[0], refs[1], refs[2], refs[3:G + 2], refs[G + 2:]
    nd, lanes = tile_sizes(rows, G)
    first = (far_stats,) + tuple(scratch[:6])
    far_stats[...] = last[0][...]
    finish_tile(0, r0, rows, G, parts, shared, products, first, scratch[6:])
    partner, per = G // 2, H // TILES
    for j in range(H):
        att, gq = (first, last)[j // per][1:3]
        for e, ref in enumerate((out_own, out_swap[partner - 1])):
            lo = (2 * (j % per) + e) * rows
            ref[j, 0:rows] = att[lo:lo + rows]
            ref[j, rows:2 * rows] = gq[lo:lo + rows]
        for g in range(G):
            at = pl.ds((j * G + g) * rows, rows)
            gk1, gk2, gv1, gv2 = (last[3 + i][at] + first[3 + i][at] if j < per else last[3 + i][at] for i in range(4))
            ref = out_kv if g == 0 else out_swap[g - 1]
            base = 2 if g == partner else 0
            for i, part in enumerate((gk2 * SCALE, gv2, gk1 * SCALE, gv1), base):
                ref[j, i * rows:(i + 1) * rows] = part.astype(ref.dtype)


def far_rows(query_refs, g, members, u, rows, lo):
    pair = (query_refs[u * members + g], query_refs[u * members + (g ^ (members // 2))])
    return jnp.concatenate([ref[(2 * j + lo) * rows:(2 * j + lo + 1) * rows] for j in range(H // TILES) for ref in pair], 0)


def far_slots(members, body):
    for g in range(members):
        slot = lax.axis_index("member") ^ g

        @pl.when((lax.axis_index("half") == 0) & (slot < members // 2))
        def _(g=g, slot=slot):
            body(g, slot)


def far_kernel(r0, rows, members, own_ref, *refs):
    G = members
    query_refs, products = refs[:TILES * G], refs[TILES * G:]
    sel = selector(lax.axis_index("head"), r0, rows, HD, False)[:rows]
    per = H // TILES
    keys, values = (jnp.concatenate([own_ref[j, lo * rows:(lo + 1) * rows] for j in range(H)], 0) for lo in (6, 7))
    docs = doc_cols(jnp.concatenate([sel * own_ref[j, 8 * rows:8 * rows + DOC_ROWS][0:1] for j in range(H)], 0))

    def body(g, slot):
        for u in range(TILES):
            x0 = u * per * rows
            pair = (query_refs[u * G + g], query_refs[u * G + (g ^ (G // 2))])
            dq = jnp.concatenate([sel * ref[2 * per * rows:2 * per * rows + DOC_ROWS][j:j + 1]
                                  for j in range(per) for ref in pair], 0)
            qdoc = dot_nt(jnp.ones((16, HD), jnp.bfloat16), dq)[0:1]
            s = dot_nt(keys[x0:], far_rows(query_refs, g, G, u, rows, 0)) * (SCALE * LOG2E)
            products[2 * u][slot] = jnp.where(docs[x0:] == qdoc, s, MASKED)
            products[2 * u + 1][slot] = dot_nt(values[x0:], far_rows(query_refs, g, G, u, rows, 1))

    far_slots(G, body)


def far_grads(rows, members, query_refs, stat_ref, products, gk, gv):
    G = members
    per = H // TILES
    gk[...], gv[...] = jnp.zeros_like(gk), jnp.zeros_like(gv)

    def body(g, slot):
        for u in range(TILES):
            x0 = u * per * rows
            chunks = per * 2 * rows // HD
            lse, dot = (jnp.concatenate([stat_ref[at + i:at + i + 1] for i in range(chunks)], 1)
                        for at in (8 * g + u * chunks, 8 * g + 4 + u * chunks))
            p = jnp.exp2(products[2 * u][slot] - lse)
            ds = p * (products[2 * u + 1][slot] - dot)
            gk[x0:] += dot_nn(ds.astype(jnp.bfloat16), far_rows(query_refs, g, G, u, rows, 0)) * SCALE
            gv[x0:] += dot_nn(p.astype(jnp.bfloat16), far_rows(query_refs, g, G, u, rows, 1))

    far_slots(G, body)


def sum_kernel(rows, members, *refs):
    G = members
    query_refs, refs = refs[:TILES * G], refs[TILES * G:]
    stat_ref, products, refs = refs[0], refs[1:1 + 2 * TILES], refs[1 + 2 * TILES:]
    own_ref, kv_ref, swap_refs, (out_ref, gk, gv) = refs[0], refs[1], refs[2:G + 1], refs[G + 1:]
    f32, bf16 = jnp.float32, jnp.bfloat16
    far_grads(rows, G, query_refs, stat_ref, products, gk, gv)
    out_ref[:, 0:2 * rows] = own_ref[...]
    out_ref[:, 2 * rows:4 * rows] = swap_refs[G // 2 - 1][:, 0:2 * rows]
    for j in range(H):
        total = kv_ref[j]
        for g, ref in enumerate(swap_refs, 1):
            base = 2 * rows if g == G // 2 else 0
            total = total + ref[j, base:base + 4 * rows].astype(f32)
        mine = slice(j * rows, (j + 1) * rows)
        out_ref[j, 4 * rows:6 * rows] = total[:2 * rows].astype(bf16)
        out_ref[j, 6 * rows:7 * rows] = (total[2 * rows:3 * rows] + gk[mine]).astype(bf16)
        out_ref[j, 7 * rows:8 * rows] = (total[3 * rows:] + gv[mine]).astype(bf16)


def unpack_kernel(r0, rows, members, in_ref, *refs):
    outs, bufs, sem = refs[:4], refs[4:8], refs[8]
    tokens = bufs[0].shape[0]
    bf16 = jnp.bfloat16
    kinds = range(min(H, 2 * r0))
    query_sels = [selector(h, r0, rows, tokens, True, takes_fine(members)) for h in kinds]
    key_sels = [selector(h, r0, rows, tokens, True, True) for h in kinds]
    copies = []
    for i, base in enumerate((0, 1, 4, 5)):
        for h in range(H):
            sels = query_sels if i < 2 else key_sels
            part = jnp.concatenate([in_ref[h, (base + e) * rows:(base + e + 1) * rows] for e in (0, 2)], 0)
            bufs[i][:, h * HD:(h + 1) * HD] = dot_nn(sels[h % (2 * r0)], part).astype(bf16)
        copies.append(pltpu.make_async_copy(bufs[i], outs[i], sem.at[i]))
        copies[-1].start()
    for copy in copies:
        copy.wait()


def call(kernel, out_shape, scratch=(), limit=16, **more):
    return pl.pallas_call(
        kernel,
        out_shape=out_shape,
        scratch_shapes=list(scratch),
        compiler_params=pltpu.CompilerParams(vmem_limit_bytes=limit * 1024 * 1024),
        **more,
    )


def per_device(members, queries, keys, values, cotangent, doc_ids):
    G = members
    tokens = queries.shape[0]
    devices = 2 * H * G
    r0 = tokens * devices // (2 * SEG)
    rows = tokens // (2 * r0)
    bf16, f32 = jnp.bfloat16, jnp.float32
    shape = jax.ShapeDtypeStruct
    n = H * G * rows
    anywhere = pl.BlockSpec(memory_space=pltpu.HBM)
    wide = pltpu.VMEM((tokens, H * HD), bf16)
    message = (H, 8 * rows + DOC_ROWS, HD)

    packed = call(
        functools.partial(pack_kernel, r0, rows, G), shape(message, bf16),
        [wide] * 4 + [pltpu.VMEM((1, tokens), jnp.int32), pltpu.VMEM(message, bf16), pltpu.SemaphoreType.DMA((5 + H,))],
        limit=64, in_specs=[anywhere] * 5, out_specs=anywhere,
    )(queries, keys, values, cotangent, doc_ids.reshape(1, tokens))

    def to_head(x):
        return lax.all_to_all(x, "head", 0, 0, tiled=True)

    def to_member(x, g):
        return lax.ppermute(x, "member", [(i, i ^ g) for i in range(G)])

    def across(x):
        return lax.ppermute(x, "half", [(0, 1), (1, 0)])

    own = to_head(packed)
    queries_here = jnp.where(takes_fine(G), own[:, 2 * rows:4 * rows], own[:, :2 * rows])
    sent_across = jnp.where(lax.axis_index("half") == 0, own[:, 6 * rows:8 * rows], queries_here)
    per = H // TILES

    def part_across(u):
        at = slice(u * per, (u + 1) * per)
        docs = jnp.pad(own[at, 8 * rows], ((0, DOC_ROWS - per), (0, 0)))
        return across(jnp.concatenate([sent_across[at].reshape(-1, HD), docs], 0))

    upper, lower = part_across(1), part_across(0)
    swaps = [to_member(own[:, (2 if g == G // 2 else 4) * rows:], g) for g in range(1, G)]
    nd, lanes = tile_sizes(rows, G)
    nq = TILES * lanes
    tile = [shape(((u + 1) * nd, lanes), f32) for u in range(TILES) for _ in range(2)]
    key_rows = pltpu.VMEM((n, HD), bf16)
    k1, k2, q_all, g_all, stats, out, gtt, *products = call(
        functools.partial(local_kernel, r0, rows, G),
        [shape((n, HD), bf16)] * 2 + [shape((nq, HD), bf16)] * 2 + [shape((8, nq), f32)]
        + [shape((HD, nq), f32)] * 2 + tile * 2,
        [key_rows] * 4, limit=32,
    )(own, *swaps)
    shared = (q_all, g_all, stats, out, gtt, k1, k2)
    upper, k1 = lax.optimization_barrier((upper, k1))
    uppers = [upper] + [to_member(upper, g) for g in range(1, G)]
    tile_rows = pltpu.VMEM((lanes, HD), bf16)
    far_scratch = lambda keys: [pltpu.VMEM((keys, HD), bf16)] * 3
    last = call(
        functools.partial(last_tile_kernel, r0, rows, G),
        [shape((8, HD), f32)] + [shape((lanes, HD), bf16)] * 2 + [shape((n, HD), f32)] * 4,
        far_scratch(nd), limit=32,
    )(*uppers, *shared, *products[2:4], *products[6:8])
    lowers = [lower] + [to_member(lower, g) for g in range(1, G)]
    sent = lambda g: (H, (6 if g == G // 2 else 4) * rows, HD)
    outs = call(
        functools.partial(first_tile_kernel, r0, rows, G),
        [shape((8, HD), f32), shape((H, 2 * rows, HD), bf16), shape((H, 4 * rows, HD), f32)]
        + [shape(sent(g), bf16) for g in range(1, G)],
        [tile_rows] * 2 + [pltpu.VMEM((nd, HD), f32)] * 4 + far_scratch(n), limit=32,
    )(*lowers, *uppers, *shared, *products[0:2], *products[4:6], *last)
    crosses = lowers + uppers
    far_stats = across(jnp.concatenate([outs[0]] + [to_member(outs[0], g) for g in range(1, G)], 0))
    products = call(
        functools.partial(far_kernel, r0, rows, G),
        [shape((G // 2, (TILES - u) * nd // G, lanes), f32) for u in range(TILES) for _ in range(2)],
    )(own, *crosses)
    swaps = [to_member(outs[2 + g], g) for g in range(1, G)]
    back = call(
        functools.partial(sum_kernel, rows, G), shape((H, 8 * rows, HD), bf16),
        [pltpu.VMEM((H * rows, HD), f32)] * 2,
    )(*crosses, far_stats, *products, outs[1], outs[2], *swaps)
    back = to_head(back)
    return tuple(call(
        functools.partial(unpack_kernel, r0, rows, G), [shape((tokens, H * HD), bf16)] * 4,
        [wide] * 4 + [pltpu.SemaphoreType.DMA((4,))],
        in_specs=[VMEM], out_specs=[anywhere] * 4,
    )(back))


def solution(mesh):
    members = mesh.shape["seq"] // (2 * H)
    parts = {"seq": [("half", 2), ("head", H), ("member", members)]}
    axes = [part for name in mesh.axis_names for part in parts.get(name, [(name, mesh.shape[name])])]
    inner = Mesh(mesh.devices.reshape([size for _, size in axes]), [name for name, _ in axes])
    split = ("dp", "half", "head", "member")
    in_specs = (P(split, None),) * 4 + (P(split),)
    return jax.shard_map(
        functools.partial(per_device, members), mesh=inner, in_specs=in_specs,
        out_specs=(P(split, None),) * 4, check_vma=False,
    )
```

profile of v0, /device:TPU:0, one launch (start us, length us, event | category | flops | bytes accessed | tf_op | source)
XLA Modules:
  0.0 50.4 jit_solution(13279644043722183147)
XLA Ops:
  0.6 2.3 %shard_map.84 = bf16[8,272,128]{2,1,0:T(8,128)(2,1)} custom-call(bf16[128,1024]{1,0:T(8,128)(2,1)} %q_in.1, bf16[128,1024]{1,0:T(8,128)(2,1)} %k_in.1, bf16[128,1024]{1,0:T(8,128)(2,1)} %v_in.1, bf16[128,1024]{1,0:T(8,128)(2,1)} %g_in.1, s32[1,128]{1,0:T(1,128)} %bitcast.13), custom_call_target="tpu_custom_call" | custom-call | tf_op jit(solution)/shard_map/pallas_call | solution.py:391
  3.0 6.2 %all-to-all-start = ((bf16[8,272,128]{2,1,0:T(8,128)(2,1)}), bf16[8,272,128]{2,1,0:T(8,128)(2,1)S(1)}, u32[]{:S(2)}, u32[]{:S(2)}) async-start(bf16[8,272,128]{2,1,0:T(8,128)(2,1)} %shard_map.84), calls=%async_computation | async-start | bytes 1114112 | tf_op jit(solution)/shard_map/all_to_all | solution.py:398
  9.2 9.4 %all-to-all-done.refs_0_.own_ref = bf16[8,272,128]{2,1,0:T(8,128)(2,1)S(1)} async-done(((bf16[8,272,128]{2,1,0:T(8,128)(2,1)}), bf16[8,272,128]{2,1,0:T(8,128)(2,1)S(1)}, u32[]{:S(2)}, u32[]{:S(2)}) %all-to-all-start) | async-done | bytes 557088 | tf_op jit(solution)/shard_map/all_to_all | solution.py:398
  18.7 0.1 collective-permute-start.3
  18.8 2.7 %collective-permute-start.2 = (bf16[272,128]{1,0:T(8,128)(2,1)S(1)}, bf16[272,128]{1,0:T(8,128)(2,1)S(1)}, u32[]{:S(2)}, u32[]{:S(2)}) collective-permute-start(bf16[272,128]{1,0:T(8,128)(2,1)S(1)} %fusion.4), channel_id=1, source_target_pairs={{0,16},{16,0},{1,17},{17,1},{2,18},{18,2},{3,19},{19,3},{4,20},{20... | collective-permute-start | bytes 208904 | tf_op jit(solution)/shard_map/ppermute | solution.py:404
  21.5 0.3 collective-permute-start
  21.8 0.0 collective-permute-done.3.refs_1_
  21.8 1.6 %shard_map.85 = (bf16[512,128]{1,0:T(8,128)(2,1)S(1)}, bf16[512,128]{1,0:T(8,128)(2,1)S(1)}, bf16[512,128]{1,0:T(8,128)(2,1)S(1)}, bf16[512,128]{1,0:T(8,128)(2,...) custom-call(bf16[8,272,128]{2,1,0:T(8,128)(2,1)S(1)} %all-to-all-don, ...), custom_call_target="tpu_custom_call" | custom-call | tf_op jit(solution)/shard_map/pallas_call | solution.py:422
  23.5 4.3 %collective-permute-done.2.refs_0_.refs_2_ = bf16[272,128]{1,0:T(8,128)(2,1)S(1)} collective-permute-done((bf16[272,128]{1,0:T(8,128)(2,1)S(1)}, bf16[272,128]{1,0:T(8,128)(2,1)S(1)}, u32[]{:S(2)}, u32[]{:S(2)}) %collective-permute-start.2) | collective-permute-done | bytes 69664 | tf_op jit(solution)/shard_map/ppermute | solution.py:404
  27.7 1.1 %collective-permute-done.refs_0_ = bf16[272,128]{1,0:T(8,128)(2,1)S(1)} collective-permute-done((bf16[272,128]{1,0:T(8,128)(2,1)S(1)}, bf16[272,128]{1,0:T(8,128)(2,1)S(1)}, u32[]{:S(2)}, u32[]{:S(2)}) %collective-permute-start) | collective-permute-done | bytes 69664 | tf_op jit(solution)/shard_map/ppermute | solution.py:404
  28.8 0.0 collective-permute-start.1
  28.8 0.2 collective-permute-done.4.refs_1_.refs_3_
  29.0 0.8 %shard_map.86 = (f32[8,128]{1,0:T(8,128)S(1)}, bf16[256,128]{1,0:T(8,128)(2,1)S(1)}, bf16[256,128]{1,0:T(8,128)(2,1)S(1)}, f32[512,128]{1,0:T(8,128)S(1)}, f32[5...) custom-call(bf16[272,128]{1,0:T(8,128)(2,1)S(1)} %collective-permute-done.2.refs_0_.refs_2_, ...), custom_call_target="tpu_custom_call" | custom-call | tf_op jit(solution)/shard_map/pallas_call | solution.py:433
  29.8 0.3 collective-permute-done.1.refs_1_
  30.1 0.6 %shard_map.87 = (f32[8,128]{1,0:T(8,128)S(1)}, bf16[8,64,128]{2,1,0:T(8,128)(2,1)S(1)}, f32[8,128,128]{2,1,0:T(8,128)S(1)}, bf16[8,192,128]{2,1,0:T(8,128)(2,1)S(1)}) custom-call(bf16[272,128]{1,0:T(8,128)(2,1)S(1)} %collective-permute-done.refs_0_, bf16[272,128]{1,0:T(8,128)(2,1)S(1)} %collective-permute-done.1.refs_1_, ...), custom_call_target="tpu_custom_call" | custom-call | tf_op jit(solution)/shard_map/pallas_call | solution.py:440
  30.7 0.2 collective-permute-start.7
  30.9 0.4 collective-permute-start.5
  31.3 1.2 %collective-permute-done.5 = f32[8,128]{1,0:T(8,128)S(1)} collective-permute-done((f32[8,128]{1,0:T(8,128)S(1)}, f32[8,128]{1,0:T(8,128)S(1)}, u32[]{:S(2)}, u32[]{:S(2)}) %collective-permute-start.5) | collective-permute-done | bytes 4128 | tf_op jit(solution)/shard_map/ppermute | solution.py:401
  32.5 0.5 collective-permute-start.6
  33.0 0.4 shard_map.88
  33.4 3.6 %collective-permute-done.6.refs_4_ = f32[16,128]{1,0:T(8,128)S(1)} collective-permute-done((f32[16,128]{1,0:T(8,128)S(1)}, f32[16,128]{1,0:T(8,128)S(1)}, u32[]{:S(2)}, u32[]{:S(2)}) %collective-permute-start.6) | collective-permute-done | bytes 8224 | tf_op jit(solution)/shard_map/ppermute | solution.py:404
  37.0 0.3 shard_map.89
  37.4 11.7 %all_to_all.10.in_ref = bf16[8,256,128]{2,1,0:T(8,128)(2,1)S(1)} all-to-all(bf16[8,256,128]{2,1,0:T(8,128)(2,1)S(1)} %shard_map.89), channel_id=1, replica_groups=mesh['half'=2,'head'=8,'member'=2,'dp'=1] {'head'}, dimensions={0} | all-to-all | bytes 1048576 | tf_op jit(solution)/shard_map/all_to_all | solution.py:398
  49.1 1.3 %shard_map.90 = (bf16[128,1024]{1,0:T(8,128)(2,1)}, bf16[128,1024]{1,0:T(8,128)(2,1)}, bf16[128,1024]{1,0:T(8,128)(2,1)}, bf16[128,1024]{1,0:T(8,128)(2,1)}) custom-call(bf16[8,256,128]{2,1,0:T(8,128)(2,1)S(1)} %all_to_all.10.in_ref), custom_call_target="tpu_custom_call" | custom-call | tf_op jit(solution)/shard_map/pallas_call | solution.py:458
  (11 shorter events, 0.1 us)
Async XLA Ops:
  3.0 15.6 %all-to-all-start = ((bf16[8,272,128]{2,1,0:T(8,128)(2,1)}), bf16[8,272,128]{2,1,0:T(8,128)(2,1)S(1)}, u32[]{:S(2)}, u32[]{:S(2)}) async-start(bf16[8,272,128]{2,1,0:T(8,128)(2,1)} %shard_map.84), calls=%async_computation | async-start | bytes 1114112 | tf_op jit(solution)/shard_map/all_to_all | solution.py:398
  18.7 3.1 %collective-permute-start.3 = (bf16[8,208,128]{2,1,0:T(8,128)(2,1)S(1)}, bf16[8,208,128]{2,1,0:T(8,128)(2,1)S(1)}, u32[]{:S(2)}, u32[]{:S(2)}) collective-permute-start(bf16[8,208,128]{2,1,0:T(8,128)(2,1)S(1)} %slice.39), channel_id=1, source_target_pairs={{0,1},{1,0},{2,3},{3,2},{4,5},{5,4},{6,7},{7,6},{8,9},{9,8},{10,11... | collective-permute-start | bytes 1277960 | tf_op jit(solution)/shard_map/ppermute | solution.py:401
  18.8 8.9 %collective-permute-start.2 = (bf16[272,128]{1,0:T(8,128)(2,1)S(1)}, bf16[272,128]{1,0:T(8,128)(2,1)S(1)}, u32[]{:S(2)}, u32[]{:S(2)}) collective-permute-start(bf16[272,128]{1,0:T(8,128)(2,1)S(1)} %fusion.4), channel_id=1, source_target_pairs={{0,16},{16,0},{1,17},{17,1},{2,18},{18,2},{3,19},{19,3},{4,20},{20... | collective-permute-start | bytes 208904 | tf_op jit(solution)/shard_map/ppermute | solution.py:404
  21.5 7.4 %collective-permute-start = (bf16[272,128]{1,0:T(8,128)(2,1)S(1)}, bf16[272,128]{1,0:T(8,128)(2,1)S(1)}, u32[]{:S(2)}, u32[]{:S(2)}) collective-permute-start(bf16[272,128]{1,0:T(8,128)(2,1)S(1)} %fusion.3), channel_id=1, source_target_pairs={{0,16},{16,0},{1,17},{17,1},{2,18},{18,2},{3,19},{19,3},{4,20},{20... | collective-permute-start | bytes 208904 | tf_op jit(solution)/shard_map/ppermute | solution.py:404
  27.7 1.3 %collective-permute-start.4 = (bf16[272,128]{1,0:T(8,128)(2,1)S(1)}, bf16[272,128]{1,0:T(8,128)(2,1)S(1)}, u32[]{:S(2)}, u32[]{:S(2)}) collective-permute-start(bf16[272,128]{1,0:T(8,128)(2,1)S(1)} %collective-permute-done.2.refs_0_.refs_2_), channel_id=1, source_target_pairs={{0,1},{1,0},{2,3},{3,2},{4,5},{5,4},{6,7},{7,6},{8,9},{9,8},{10,11... | collective-permute-start | bytes 208904 | tf_op jit(solution)/shard_map/ppermute | solution.py:401
  28.8 1.3 %collective-permute-start.1 = (bf16[272,128]{1,0:T(8,128)(2,1)S(1)}, bf16[272,128]{1,0:T(8,128)(2,1)S(1)}, u32[]{:S(2)}, u32[]{:S(2)}) collective-permute-start(bf16[272,128]{1,0:T(8,128)(2,1)S(1)} %collective-permute-done.refs_0_), channel_id=1, source_target_pairs={{0,1},{1,0},{2,3},{3,2},{4,5},{5,4},{6,7},{7,6},{8,9},{9,8},{10,11... | collective-permute-start | bytes 208904 | tf_op jit(solution)/shard_map/ppermute | solution.py:401
  30.7 6.3 %collective-permute-start.7 = (bf16[8,192,128]{2,1,0:T(8,128)(2,1)S(1)}, bf16[8,192,128]{2,1,0:T(8,128)(2,1)S(1)}, u32[]{:S(2)}, u32[]{:S(2)}) collective-permute-start(bf16[8,192,128]{2,1,0:T(8,128)(2,1)S(1)} %get-tuple-element.65), channel_id=1, source_target_pairs={{0,1},{1,0},{2,3},{3,2},{4,5},{5,4},{6,7},{7,6},{8,9},{9,8},{10,11... | collective-permute-start | bytes 1179656 | tf_op jit(solution)/shard_map/ppermute | solution.py:401
  30.9 1.6 %collective-permute-start.5 = (f32[8,128]{1,0:T(8,128)S(1)}, f32[8,128]{1,0:T(8,128)S(1)}, u32[]{:S(2)}, u32[]{:S(2)}) collective-permute-start(f32[8,128]{1,0:T(8,128)S(1)} %get-tuple-element.58), channel_id=1, source_target_pairs={{0,1},{1,0},{2,3},{3,2},{4,5},{5,4},{6,7},{7,6},{8,9},{9,8},{10,11... | collective-permute-start | bytes 12296 | tf_op jit(solution)/shard_map/ppermute | solution.py:401
  32.5 4.5 %collective-permute-start.6 = (f32[16,128]{1,0:T(8,128)S(1)}, f32[16,128]{1,0:T(8,128)S(1)}, u32[]{:S(2)}, u32[]{:S(2)}) collective-permute-start(f32[16,128]{1,0:T(8,128)S(1)} %pad_maximum_fusion), channel_id=1, source_target_pairs={{0,16},{16,0},{1,17},{17,1},{2,18},{18,2},{3,19},{19,3},{4,20},{20... | collective-permute-start | bytes 24584 | tf_op jit(solution)/shard_map/ppermute | solution.py:404
where the time goes:
time: 50.6 us; the launch traced here: 50.4 us
  waiting for transfers between devices  20.1 us (40%)
  blocking collectives  11.7 us (23%)
  starting transfers between devices  10.3 us (20%)
  Pallas kernels  7.41 us (15%)
  between operations  0.73 us (1%)
    all_to_all x1, blocking collectives, to_head(): return lax.all_to_all(x, 'head', 0, 0, tiled=True)  11.7 us
    all_to_all x1, waiting for transfers between devices, to_head(): return lax.all_to_all(x, 'head', 0, 0, tiled=True)  9.42 us
    ppermute x3, waiting for transfers between devices, across(): return lax.ppermute(x, 'half', [(0, 1), (1, 0)])  8.96 us
    all_to_all x1, starting transfers between devices, to_head(): return lax.all_to_all(x, 'head', 0, 0, tiled=True)  6.2 us
    ppermute x3, starting transfers between devices, across(): return lax.ppermute(x, 'half', [(0, 1), (1, 0)])  3.49 us
    pallas_call x1, Pallas kernels, per_device(): call(functools.partial(pack_kernel, r0, rows, G), shape(message, bf16), [...  2.35 us
    ppermute x5, waiting for transfers between devices, to_member(): return lax.ppermute(x, 'member', [(i, i ^ g) for i in range(G)])  1.72 us
    pallas_call x1, Pallas kernels, per_device(): call(functools.partial(local_kernel, r0, rows, G), [shape((n, HD), bf16)]...  1.65 us
  transfers between devices with their start and end apart: 9, of which 7 were waited for; matrix products, arithmetic and copies ran while one was open for 0% of the time, Pallas kernels for 6%

commit v1 on v0

--- a/solution.py
+++ b/solution.py
@@ -44,11 +44,18 @@
     return lax.axis_index("member") >= members // 2
 
 
+def column_chunks():
+    return [((h, h + 1), slice(h * HD, (h + 2) * HD)) for h in range(0, H, 2)]
+
+
 def pack_kernel(r0, rows, members, q_in, k_in, v_in, g_in, doc_in, out, q_ref, k_ref, v_ref, g_ref, doc_ref, buf, sem):
     tokens = q_ref.shape[0]
-    pairs = ((doc_in, doc_ref), (k_in, k_ref), (v_in, v_ref), (q_in, q_ref), (g_in, g_ref))
-    copies = [pltpu.make_async_copy(src, dst, sem.at[i]) for i, (src, dst) in enumerate(pairs)]
-    for copy in copies:
+    pairs = ((q_in, q_ref), (g_in, g_ref), (k_in, k_ref), (v_in, v_ref))
+    copies = [[pltpu.make_async_copy(doc_in, doc_ref, sem.at[0])]]
+    for i, (_, cols) in enumerate(column_chunks()):
+        copies.append([pltpu.make_async_copy(src.at[:, cols], dst.at[:, cols], sem.at[1 + 4 * i + k])
+                       for k, (src, dst) in enumerate(pairs)])
+    for copy in sum(copies, []):
         copy.start()
     kinds = range(min(H, 2 * r0))
     key_sels = [selector(h, r0, rows, tokens, False) for h in kinds]
@@ -57,22 +64,24 @@
     def pick(sels, h, ref):
         return dot_nn(sels[h % (2 * r0)], ref[:, h * HD:(h + 1) * HD]).astype(jnp.bfloat16)
 
-    for copy in copies:
-        copy.wait()
+    copies[0][0].wait()
     docs = jnp.broadcast_to(doc_ref[...].astype(jnp.float32).astype(jnp.bfloat16), (DOC_ROWS, tokens))
     sends = []
-    for h in range(H):
-        for i, ref in enumerate((q_ref, g_ref)):
-            x = pick(query_sels, h, ref)
-            buf[h, i * rows:(1 + i) * rows] = x[:rows]
-            buf[h, (2 + i) * rows:(3 + i) * rows] = x[rows:]
-        for i, ref in enumerate((k_ref, v_ref)):
-            x = pick(key_sels, h, ref)
-            buf[h, (4 + i) * rows:(5 + i) * rows] = x[rows:]
-            buf[h, (6 + i) * rows:(7 + i) * rows] = x[:rows]
-        buf[h, 8 * rows:8 * rows + DOC_ROWS] = docs
-        sends.append(pltpu.make_async_copy(buf.at[h], out.at[h], sem.at[5 + h]))
-        sends[-1].start()
+    for group, (heads, _) in zip(copies[1:], column_chunks()):
+        for copy in group:
+            copy.wait()
+        for h in heads:
+            for i, ref in enumerate((q_ref, g_ref)):
+                x = pick(query_sels, h, ref)
+                buf[h, i * rows:(1 + i) * rows] = x[:rows]
+                buf[h, (2 + i) * rows:(3 + i) * rows] = x[rows:]
+            for i, ref in enumerate((k_ref, v_ref)):
+                x = pick(key_sels, h, ref)
+                buf[h, (4 + i) * rows:(5 + i) * rows] = x[rows:]
+                buf[h, (6 + i) * rows:(7 + i) * rows] = x[:rows]
+            buf[h, 8 * rows:8 * rows + DOC_ROWS] = docs
+            sends.append(pltpu.make_async_copy(buf.at[h], out.at[h], sem.at[1 + 2 * H + h]))
+            sends[-1].start()
     for copy in sends:
         copy.wait()
 
@@ -354,13 +363,14 @@
     query_sels = [selector(h, r0, rows, tokens, True, takes_fine(members)) for h in kinds]
     key_sels = [selector(h, r0, rows, tokens, True, True) for h in kinds]
     copies = []
-    for i, base in enumerate((0, 1, 4, 5)):
-        for h in range(H):
+    for heads, cols in column_chunks():
+        for i, base in enumerate((0, 1, 4, 5)):
             sels = query_sels if i < 2 else key_sels
-            part = jnp.concatenate([in_ref[h, (base + e) * rows:(base + e + 1) * rows] for e in (0, 2)], 0)
-            bufs[i][:, h * HD:(h + 1) * HD] = dot_nn(sels[h % (2 * r0)], part).astype(bf16)
-        copies.append(pltpu.make_async_copy(bufs[i], outs[i], sem.at[i]))
-        copies[-1].start()
+            for h in heads:
+                part = jnp.concatenate([in_ref[h, (base + e) * rows:(base + e + 1) * rows] for e in (0, 2)], 0)
+                bufs[i][:, h * HD:(h + 1) * HD] = dot_nn(sels[h % (2 * r0)], part).astype(bf16)
+            copies.append(pltpu.make_async_copy(bufs[i].at[:, cols], outs[i].at[:, cols], sem.at[len(copies)]))
+            copies[-1].start()
     for copy in copies:
         copy.wait()
 
@@ -390,7 +400,7 @@
 
     packed = call(
         functools.partial(pack_kernel, r0, rows, G), shape(message, bf16),
-        [wide] * 4 + [pltpu.VMEM((1, tokens), jnp.int32), pltpu.VMEM(message, bf16), pltpu.SemaphoreType.DMA((5 + H,))],
+        [wide] * 4 + [pltpu.VMEM((1, tokens), jnp.int32), pltpu.VMEM(message, bf16), pltpu.SemaphoreType.DMA((1 + 3 * H,))],
         limit=64, in_specs=[anywhere] * 5, out_specs=anywhere,
     )(queries, keys, values, cotangent, doc_ids.reshape(1, tokens))
 
@@ -457,7 +467,7 @@
     back = to_head(back)
     return tuple(call(
         functools.partial(unpack_kernel, r0, rows, G), [shape((tokens, H * HD), bf16)] * 4,
-        [wide] * 4 + [pltpu.SemaphoreType.DMA((4,))],
+        [wide] * 4 + [pltpu.SemaphoreType.DMA((2 * H,))],
         in_specs=[VMEM], out_specs=[anywhere] * 4,
     )(back))
 

time: 50.6 us -> 50.9 us (level)
  no operation moved by 1% of the time
where the time goes in v1:
time: 50.9 us; the launch traced here: 50.7 us
  waiting for transfers between devices  20.1 us (39%)
  blocking collectives  11.7 us (23%)
  starting transfers between devices  10.3 us (20%)
  Pallas kernels  7.68 us (15%)
  between operations  0.73 us (1%)
    all_to_all x1, blocking collectives, to_head(): return lax.all_to_all(x, 'head', 0, 0, tiled=True)  11.7 us
    all_to_all x1, waiting for transfers between devices, to_head(): return lax.all_to_all(x, 'head', 0, 0, tiled=True)  9.42 us
    ppermute x3, waiting for transfers between devices, across(): return lax.ppermute(x, 'half', [(0, 1), (1, 0)])  8.96 us
    all_to_all x1, starting transfers between devices, to_head(): return lax.all_to_all(x, 'head', 0, 0, tiled=True)  6.19 us
    ppermute x3, starting transfers between devices, across(): return lax.ppermute(x, 'half', [(0, 1), (1, 0)])  3.49 us
    pallas_call x1, Pallas kernels, per_device(): call(functools.partial(pack_kernel, r0, rows, G), shape(message, bf16), [...  2.64 us
    ppermute x5, waiting for transfers between devices, to_member(): return lax.ppermute(x, 'member', [(i, i ^ g) for i in range(G)])  1.72 us
    pallas_call x1, Pallas kernels, per_device(): call(functools.partial(local_kernel, r0, rows, G), [shape((n, HD), bf16)]...  1.66 us
  transfers between devices with their start and end apart: 9, of which 7 were waited for; matrix products, arithmetic and copies ran while one was open for 0% of the time, Pallas kernels for 6%

profile of v1, /device:TPU:0, one launch (start us, length us, event | category | flops | bytes accessed | tf_op | source)
XLA Modules:
  0.0 50.7 jit_solution(12704336605763976135)
XLA Ops:
  0.6 2.6 %shard_map.84 = bf16[8,272,128]{2,1,0:T(8,128)(2,1)} custom-call(bf16[128,1024]{1,0:T(8,128)(2,1)} %q_in.1, bf16[128,1024]{1,0:T(8,128)(2,1)} %k_in.1, bf16[128,1024]{1,0:T(8,128)(2,1)} %v_in.1, bf16[128,1024]{1,0:T(8,128)(2,1)} %g_in.1, s32[1,128]{1,0:T(1,128)} %bitcast.13), custom_call_target="tpu_custom_call" | custom-call | tf_op jit(solution)/shard_map/pallas_call | solution.py:401
  3.3 6.2 %all-to-all-start = ((bf16[8,272,128]{2,1,0:T(8,128)(2,1)}), bf16[8,272,128]{2,1,0:T(8,128)(2,1)S(1)}, u32[]{:S(2)}, u32[]{:S(2)}) async-start(bf16[8,272,128]{2,1,0:T(8,128)(2,1)} %shard_map.84), calls=%async_computation | async-start | bytes 1114112 | tf_op jit(solution)/shard_map/all_to_all | solution.py:408
  9.5 9.4 %all-to-all-done.refs_0_.own_ref = bf16[8,272,128]{2,1,0:T(8,128)(2,1)S(1)} async-done(((bf16[8,272,128]{2,1,0:T(8,128)(2,1)}), bf16[8,272,128]{2,1,0:T(8,128)(2,1)S(1)}, u32[]{:S(2)}, u32[]{:S(2)}) %all-to-all-start) | async-done | bytes 557088 | tf_op jit(solution)/shard_map/all_to_all | solution.py:408
  19.0 0.1 collective-permute-start.3
  19.1 2.7 %collective-permute-start.2 = (bf16[272,128]{1,0:T(8,128)(2,1)S(1)}, bf16[272,128]{1,0:T(8,128)(2,1)S(1)}, u32[]{:S(2)}, u32[]{:S(2)}) collective-permute-start(bf16[272,128]{1,0:T(8,128)(2,1)S(1)} %fusion.4), channel_id=1, source_target_pairs={{0,16},{16,0},{1,17},{17,1},{2,18},{18,2},{3,19},{19,3},{4,20},{20... | collective-permute-start | bytes 208904 | tf_op jit(solution)/shard_map/ppermute | solution.py:414
  21.8 0.3 collective-permute-start
  22.1 1.7 %shard_map.85 = (bf16[512,128]{1,0:T(8,128)(2,1)S(1)}, bf16[512,128]{1,0:T(8,128)(2,1)S(1)}, bf16[512,128]{1,0:T(8,128)(2,1)S(1)}, bf16[512,128]{1,0:T(8,128)(2,...) custom-call(bf16[8,272,128]{2,1,0:T(8,128)(2,1)S(1)} %all-to-all-don, ...), custom_call_target="tpu_custom_call" | custom-call | tf_op jit(solution)/shard_map/pallas_call | solution.py:432
  23.8 4.3 %collective-permute-done.2.refs_0_.refs_2_ = bf16[272,128]{1,0:T(8,128)(2,1)S(1)} collective-permute-done((bf16[272,128]{1,0:T(8,128)(2,1)S(1)}, bf16[272,128]{1,0:T(8,128)(2,1)S(1)}, u32[]{:S(2)}, u32[]{:S(2)}) %collective-permute-start.2) | collective-permute-done | bytes 69664 | tf_op jit(solution)/shard_map/ppermute | solution.py:414
  28.0 0.0 collective-permute-start.4
  28.0 1.1 %collective-permute-done.refs_0_ = bf16[272,128]{1,0:T(8,128)(2,1)S(1)} collective-permute-done((bf16[272,128]{1,0:T(8,128)(2,1)S(1)}, bf16[272,128]{1,0:T(8,128)(2,1)S(1)}, u32[]{:S(2)}, u32[]{:S(2)}) %collective-permute-start) | collective-permute-done | bytes 69664 | tf_op jit(solution)/shard_map/ppermute | solution.py:414
  29.1 0.0 collective-permute-start.1
  29.1 0.2 collective-permute-done.4.refs_1_.refs_3_
  29.3 0.8 %shard_map.86 = (f32[8,128]{1,0:T(8,128)S(1)}, bf16[256,128]{1,0:T(8,128)(2,1)S(1)}, bf16[256,128]{1,0:T(8,128)(2,1)S(1)}, f32[512,128]{1,0:T(8,128)S(1)}, f32[5...) custom-call(bf16[272,128]{1,0:T(8,128)(2,1)S(1)} %collective-permute-done.2.refs_0_.refs_2_, ...), custom_call_target="tpu_custom_call" | custom-call | tf_op jit(solution)/shard_map/pallas_call | solution.py:443
  30.1 0.3 collective-permute-done.1.refs_1_
  30.4 0.6 %shard_map.87 = (f32[8,128]{1,0:T(8,128)S(1)}, bf16[8,64,128]{2,1,0:T(8,128)(2,1)S(1)}, f32[8,128,128]{2,1,0:T(8,128)S(1)}, bf16[8,192,128]{2,1,0:T(8,128)(2,1)S(1)}) custom-call(bf16[272,128]{1,0:T(8,128)(2,1)S(1)} %collective-permute-done.refs_0_, bf16[272,128]{1,0:T(8,128)(2,1)S(1)} %collective-permute-done.1.refs_1_, ...), custom_call_target="tpu_custom_call" | custom-call | tf_op jit(solution)/shard_map/pallas_call | solution.py:450
  31.0 0.2 collective-permute-start.7
  31.2 0.4 collective-permute-start.5
  31.6 1.2 %collective-permute-done.5 = f32[8,128]{1,0:T(8,128)S(1)} collective-permute-done((f32[8,128]{1,0:T(8,128)S(1)}, f32[8,128]{1,0:T(8,128)S(1)}, u32[]{:S(2)}, u32[]{:S(2)}) %collective-permute-start.5) | collective-permute-done | bytes 4128 | tf_op jit(solution)/shard_map/ppermute | solution.py:411
  32.8 0.5 collective-permute-start.6
  33.3 0.4 shard_map.88
  33.7 3.6 %collective-permute-done.6.refs_4_ = f32[16,128]{1,0:T(8,128)S(1)} collective-permute-done((f32[16,128]{1,0:T(8,128)S(1)}, f32[16,128]{1,0:T(8,128)S(1)}, u32[]{:S(2)}, u32[]{:S(2)}) %collective-permute-start.6) | collective-permute-done | bytes 8224 | tf_op jit(solution)/shard_map/ppermute | solution.py:414
  37.3 0.3 shard_map.89
  37.7 11.7 %all_to_all.10.in_ref = bf16[8,256,128]{2,1,0:T(8,128)(2,1)S(1)} all-to-all(bf16[8,256,128]{2,1,0:T(8,128)(2,1)S(1)} %shard_map.89), channel_id=1, replica_groups=mesh['half'=2,'head'=8,'member'=2,'dp'=1] {'head'}, dimensions={0} | all-to-all | bytes 1048576 | tf_op jit(solution)/shard_map/all_to_all | solution.py:408
  49.4 1.2 %shard_map.90 = (bf16[128,1024]{1,0:T(8,128)(2,1)}, bf16[128,1024]{1,0:T(8,128)(2,1)}, bf16[128,1024]{1,0:T(8,128)(2,1)}, bf16[128,1024]{1,0:T(8,128)(2,1)}) custom-call(bf16[8,256,128]{2,1,0:T(8,128)(2,1)S(1)} %all_to_all.10.in_ref), custom_call_target="tpu_custom_call" | custom-call | tf_op jit(solution)/shard_map/pallas_call | solution.py:468
  (11 shorter events, 0.1 us)
Async XLA Ops:
  3.3 15.6 %all-to-all-start = ((bf16[8,272,128]{2,1,0:T(8,128)(2,1)}), bf16[8,272,128]{2,1,0:T(8,128)(2,1)S(1)}, u32[]{:S(2)}, u32[]{:S(2)}) async-start(bf16[8,272,128]{2,1,0:T(8,128)(2,1)} %shard_map.84), calls=%async_computation | async-start | bytes 1114112 | tf_op jit(solution)/shard_map/all_to_all | solution.py:408
  19.0 3.1 %collective-permute-start.3 = (bf16[8,208,128]{2,1,0:T(8,128)(2,1)S(1)}, bf16[8,208,128]{2,1,0:T(8,128)(2,1)S(1)}, u32[]{:S(2)}, u32[]{:S(2)}) collective-permute-start(bf16[8,208,128]{2,1,0:T(8,128)(2,1)S(1)} %slice.39), channel_id=1, source_target_pairs={{0,1},{1,0},{2,3},{3,2},{4,5},{5,4},{6,7},{7,6},{8,9},{9,8},{10,11... | collective-permute-start | bytes 1277960 | tf_op jit(solution)/shard_map/ppermute | solution.py:411
  19.1 8.9 %collective-permute-start.2 = (bf16[272,128]{1,0:T(8,128)(2,1)S(1)}, bf16[272,128]{1,0:T(8,128)(2,1)S(1)}, u32[]{:S(2)}, u32[]{:S(2)}) collective-permute-start(bf16[272,128]{1,0:T(8,128)(2,1)S(1)} %fusion.4), channel_id=1, source_target_pairs={{0,16},{16,0},{1,17},{17,1},{2,18},{18,2},{3,19},{19,3},{4,20},{20... | collective-permute-start | bytes 208904 | tf_op jit(solution)/shard_map/ppermute | solution.py:414
  21.8 7.4 %collective-permute-start = (bf16[272,128]{1,0:T(8,128)(2,1)S(1)}, bf16[272,128]{1,0:T(8,128)(2,1)S(1)}, u32[]{:S(2)}, u32[]{:S(2)}) collective-permute-start(bf16[272,128]{1,0:T(8,128)(2,1)S(1)} %fusion.3), channel_id=1, source_target_pairs={{0,16},{16,0},{1,17},{17,1},{2,18},{18,2},{3,19},{19,3},{4,20},{20... | collective-permute-start | bytes 208904 | tf_op jit(solution)/shard_map/ppermute | solution.py:414
  28.0 1.3 %collective-permute-start.4 = (bf16[272,128]{1,0:T(8,128)(2,1)S(1)}, bf16[272,128]{1,0:T(8,128)(2,1)S(1)}, u32[]{:S(2)}, u32[]{:S(2)}) collective-permute-start(bf16[272,128]{1,0:T(8,128)(2,1)S(1)} %collective-permute-done.2.refs_0_.refs_2_), channel_id=1, source_target_pairs={{0,1},{1,0},{2,3},{3,2},{4,5},{5,4},{6,7},{7,6},{8,9},{9,8},{10,11... | collective-permute-start | bytes 208904 | tf_op jit(solution)/shard_map/ppermute | solution.py:411
  29.1 1.3 %collective-permute-start.1 = (bf16[272,128]{1,0:T(8,128)(2,1)S(1)}, bf16[272,128]{1,0:T(8,128)(2,1)S(1)}, u32[]{:S(2)}, u32[]{:S(2)}) collective-permute-start(bf16[272,128]{1,0:T(8,128)(2,1)S(1)} %collective-permute-done.refs_0_), channel_id=1, source_target_pairs={{0,1},{1,0},{2,3},{3,2},{4,5},{5,4},{6,7},{7,6},{8,9},{9,8},{10,11... | collective-permute-start | bytes 208904 | tf_op jit(solution)/shard_map/ppermute | solution.py:411
  31.0 6.3 %collective-permute-start.7 = (bf16[8,192,128]{2,1,0:T(8,128)(2,1)S(1)}, bf16[8,192,128]{2,1,0:T(8,128)(2,1)S(1)}, u32[]{:S(2)}, u32[]{:S(2)}) collective-permute-start(bf16[8,192,128]{2,1,0:T(8,128)(2,1)S(1)} %get-tuple-element.65), channel_id=1, source_target_pairs={{0,1},{1,0},{2,3},{3,2},{4,5},{5,4},{6,7},{7,6},{8,9},{9,8},{10,11... | collective-permute-start | bytes 1179656 | tf_op jit(solution)/shard_map/ppermute | solution.py:411
  31.2 1.6 %collective-permute-start.5 = (f32[8,128]{1,0:T(8,128)S(1)}, f32[8,128]{1,0:T(8,128)S(1)}, u32[]{:S(2)}, u32[]{:S(2)}) collective-permute-start(f32[8,128]{1,0:T(8,128)S(1)} %get-tuple-element.58), channel_id=1, source_target_pairs={{0,1},{1,0},{2,3},{3,2},{4,5},{5,4},{6,7},{7,6},{8,9},{9,8},{10,11... | collective-permute-start | bytes 12296 | tf_op jit(solution)/shard_map/ppermute | solution.py:411
  32.8 4.5 %collective-permute-start.6 = (f32[16,128]{1,0:T(8,128)S(1)}, f32[16,128]{1,0:T(8,128)S(1)}, u32[]{:S(2)}, u32[]{:S(2)}) collective-permute-start(f32[16,128]{1,0:T(8,128)S(1)} %pad_maximum_fusion), channel_id=1, source_target_pairs={{0,16},{16,0},{1,17},{17,1},{2,18},{18,2},{3,19},{19,3},{4,20},{20... | collective-permute-start | bytes 24584 | tf_op jit(solution)/shard_map/ppermute | solution.py:414

commit v2 on v0

--- a/solution.py
+++ b/solution.py
@@ -444,12 +444,14 @@
         [tile_rows] * 2 + [pltpu.VMEM((nd, HD), f32)] * 4 + far_scratch(n), limit=32,
     )(*lowers, *uppers, *shared, *products[0:2], *products[4:6], *last)
     crosses = lowers + uppers
-    far_stats = across(jnp.concatenate([outs[0]] + [to_member(outs[0], g) for g in range(1, G)], 0))
+    hops = [to_member(outs[0], g) for g in range(1, G)]
+    far_stats = across(jnp.concatenate([outs[0]] + hops, 0))
     products = call(
         functools.partial(far_kernel, r0, rows, G),
         [shape((G // 2, (TILES - u) * nd // G, lanes), f32) for u in range(TILES) for _ in range(2)],
     )(own, *crosses)
-    swaps = [to_member(outs[2 + g], g) for g in range(1, G)]
+    sends, _ = lax.optimization_barrier((list(outs[3:]), hops))
+    swaps = [to_member(x, g) for g, x in enumerate(sends, 1)]
     back = call(
         functools.partial(sum_kernel, rows, G), shape((H, 8 * rows, HD), bf16),
         [pltpu.VMEM((H * rows, HD), f32)] * 2,

time: 50.6 us -> 50.4 us (level)
  no operation moved by 1% of the time
where the time goes in v2:
time: 50.4 us; the launch traced here: 50.2 us
  waiting for transfers between devices  19.8 us (39%)
  blocking collectives  11.9 us (24%)
  starting transfers between devices  10.2 us (20%)
  Pallas kernels  7.42 us (15%)
  between operations  0.73 us (1%)
    all_to_all x1, blocking collectives, to_head(): return lax.all_to_all(x, 'head', 0, 0, tiled=True)  11.9 us
    all_to_all x1, waiting for transfers between devices, to_head(): return lax.all_to_all(x, 'head', 0, 0, tiled=True)  9.42 us
    ppermute x3, waiting for transfers between devices, across(): return lax.ppermute(x, 'half', [(0, 1), (1, 0)])  8.89 us
    all_to_all x1, starting transfers between devices, to_head(): return lax.all_to_all(x, 'head', 0, 0, tiled=True)  6.2 us
    ppermute x3, starting transfers between devices, across(): return lax.ppermute(x, 'half', [(0, 1), (1, 0)])  3.55 us
    pallas_call x1, Pallas kernels, per_device(): call(functools.partial(pack_kernel, r0, rows, G), shape(message, bf16), [...  2.35 us
    pallas_call x1, Pallas kernels, per_device(): call(functools.partial(local_kernel, r0, rows, G), [shape((n, HD), bf16)]...  1.66 us
    ppermute x5, waiting for transfers between devices, to_member(): return lax.ppermute(x, 'member', [(i, i ^ g) for i in range(G)])  1.51 us
  transfers between devices with their start and end apart: 9, of which 7 were waited for; matrix products, arithmetic and copies ran while one was open for 0% of the time, Pallas kernels for 6%

profile of v2, /device:TPU:0, one launch (start us, length us, event | category | flops | bytes accessed | tf_op | source)
XLA Modules:
  0.0 50.2 jit_solution(17273654829505481619)
XLA Ops:
  0.6 2.3 %shard_map.84 = bf16[8,272,128]{2,1,0:T(8,128)(2,1)} custom-call(bf16[128,1024]{1,0:T(8,128)(2,1)} %q_in.1, bf16[128,1024]{1,0:T(8,128)(2,1)} %k_in.1, bf16[128,1024]{1,0:T(8,128)(2,1)} %v_in.1, bf16[128,1024]{1,0:T(8,128)(2,1)} %g_in.1, s32[1,128]{1,0:T(1,128)} %bitcast.13), custom_call_target="tpu_custom_call" | custom-call | tf_op jit(solution)/shard_map/pallas_call | solution.py:391
  3.0 6.2 %all-to-all-start = ((bf16[8,272,128]{2,1,0:T(8,128)(2,1)}), bf16[8,272,128]{2,1,0:T(8,128)(2,1)S(1)}, u32[]{:S(2)}, u32[]{:S(2)}) async-start(bf16[8,272,128]{2,1,0:T(8,128)(2,1)} %shard_map.84), calls=%async_computation | async-start | bytes 1114112 | tf_op jit(solution)/shard_map/all_to_all | solution.py:398
  9.2 9.4 %all-to-all-done.refs_0_.own_ref = bf16[8,272,128]{2,1,0:T(8,128)(2,1)S(1)} async-done(((bf16[8,272,128]{2,1,0:T(8,128)(2,1)}), bf16[8,272,128]{2,1,0:T(8,128)(2,1)S(1)}, u32[]{:S(2)}, u32[]{:S(2)}) %all-to-all-start) | async-done | bytes 557088 | tf_op jit(solution)/shard_map/all_to_all | solution.py:398
  18.6 0.1 collective-permute-start.3
  18.8 2.7 %collective-permute-start.2 = (bf16[272,128]{1,0:T(8,128)(2,1)S(1)}, bf16[272,128]{1,0:T(8,128)(2,1)S(1)}, u32[]{:S(2)}, u32[]{:S(2)}) collective-permute-start(bf16[272,128]{1,0:T(8,128)(2,1)S(1)} %fusion.4), channel_id=1, source_target_pairs={{0,16},{16,0},{1,17},{17,1},{2,18},{18,2},{3,19},{19,3},{4,20},{20... | collective-permute-start | bytes 208904 | tf_op jit(solution)/shard_map/ppermute | solution.py:404
  21.5 0.4 collective-permute-start
  21.9 0.0 collective-permute-done.3.refs_1_
  21.9 1.7 %shard_map.85 = (bf16[512,128]{1,0:T(8,128)(2,1)S(1)}, bf16[512,128]{1,0:T(8,128)(2,1)S(1)}, bf16[512,128]{1,0:T(8,128)(2,1)S(1)}, bf16[512,128]{1,0:T(8,128)(2,...) custom-call(bf16[8,272,128]{2,1,0:T(8,128)(2,1)S(1)} %all-to-all-don, ...), custom_call_target="tpu_custom_call" | custom-call | tf_op jit(solution)/shard_map/pallas_call | solution.py:422
  23.5 4.2 %collective-permute-done.2.refs_0_.refs_2_ = bf16[272,128]{1,0:T(8,128)(2,1)S(1)} collective-permute-done((bf16[272,128]{1,0:T(8,128)(2,1)S(1)}, bf16[272,128]{1,0:T(8,128)(2,1)S(1)}, u32[]{:S(2)}, u32[]{:S(2)}) %collective-permute-start.2) | collective-permute-done | bytes 69664 | tf_op jit(solution)/shard_map/ppermute | solution.py:404
  27.7 0.0 collective-permute-start.4
  27.7 1.1 %collective-permute-done.refs_0_ = bf16[272,128]{1,0:T(8,128)(2,1)S(1)} collective-permute-done((bf16[272,128]{1,0:T(8,128)(2,1)S(1)}, bf16[272,128]{1,0:T(8,128)(2,1)S(1)}, u32[]{:S(2)}, u32[]{:S(2)}) %collective-permute-start) | collective-permute-done | bytes 69664 | tf_op jit(solution)/shard_map/ppermute | solution.py:404
  28.8 0.2 collective-permute-done.4.refs_1_.refs_3_
  29.0 0.8 %shard_map.86 = (f32[8,128]{1,0:T(8,128)S(1)}, bf16[256,128]{1,0:T(8,128)(2,1)S(1)}, bf16[256,128]{1,0:T(8,128)(2,1)S(1)}, f32[512,128]{1,0:T(8,128)S(1)}, f32[5...) custom-call(bf16[272,128]{1,0:T(8,128)(2,1)S(1)} %collective-permute-done.2.refs_0_.refs_2_, ...), custom_call_target="tpu_custom_call" | custom-call | tf_op jit(solution)/shard_map/pallas_call | solution.py:433
  29.8 0.3 collective-permute-done.1.refs_1_
  30.1 0.6 %shard_map.87 = (f32[8,128]{1,0:T(8,128)S(1)}, bf16[8,64,128]{2,1,0:T(8,128)(2,1)S(1)}, f32[8,128,128]{2,1,0:T(8,128)S(1)}, bf16[8,192,128]{2,1,0:T(8,128)(2,1)S(1)}) custom-call(bf16[272,128]{1,0:T(8,128)(2,1)S(1)} %collective-permute-done.refs_0_, bf16[272,128]{1,0:T(8,128)(2,1)S(1)} %collective-permute-done.1.refs_1_, ...), custom_call_target="tpu_custom_call" | custom-call | tf_op jit(solution)/shard_map/pallas_call | solution.py:440
  30.7 0.2 collective-permute-start.5
  30.9 1.0 %collective-permute-done.5 = f32[8,128]{1,0:T(8,128)S(1)} collective-permute-done((f32[8,128]{1,0:T(8,128)S(1)}, f32[8,128]{1,0:T(8,128)S(1)}, u32[]{:S(2)}, u32[]{:S(2)}) %collective-permute-start.5) | collective-permute-done | bytes 4128 | tf_op jit(solution)/shard_map/ppermute | solution.py:401
  31.9 0.2 collective-permute-start.7
  32.1 0.5 collective-permute-start.6
  32.6 0.4 shard_map.88
  33.0 3.6 %collective-permute-done.6.refs_4_ = f32[16,128]{1,0:T(8,128)S(1)} collective-permute-done((f32[16,128]{1,0:T(8,128)S(1)}, f32[16,128]{1,0:T(8,128)S(1)}, u32[]{:S(2)}, u32[]{:S(2)}) %collective-permute-start.6) | collective-permute-done | bytes 8224 | tf_op jit(solution)/shard_map/ppermute | solution.py:404
  36.6 0.4 shard_map.89
  37.0 11.9 %all_to_all.10.in_ref = bf16[8,256,128]{2,1,0:T(8,128)(2,1)S(1)} all-to-all(bf16[8,256,128]{2,1,0:T(8,128)(2,1)S(1)} %shard_map.89), channel_id=1, replica_groups=mesh['half'=2,'head'=8,'member'=2,'dp'=1] {'head'}, dimensions={0} | all-to-all | bytes 1048576 | tf_op jit(solution)/shard_map/all_to_all | solution.py:398
  48.9 1.3 %shard_map.90 = (bf16[128,1024]{1,0:T(8,128)(2,1)}, bf16[128,1024]{1,0:T(8,128)(2,1)}, bf16[128,1024]{1,0:T(8,128)(2,1)}, bf16[128,1024]{1,0:T(8,128)(2,1)}) custom-call(bf16[8,256,128]{2,1,0:T(8,128)(2,1)S(1)} %all_to_all.10.in_ref), custom_call_target="tpu_custom_call" | custom-call | tf_op jit(solution)/shard_map/pallas_call | solution.py:460
  (11 shorter events, 0.1 us)
Async XLA Ops:
  3.0 15.6 %all-to-all-start = ((bf16[8,272,128]{2,1,0:T(8,128)(2,1)}), bf16[8,272,128]{2,1,0:T(8,128)(2,1)S(1)}, u32[]{:S(2)}, u32[]{:S(2)}) async-start(bf16[8,272,128]{2,1,0:T(8,128)(2,1)} %shard_map.84), calls=%async_computation | async-start | bytes 1114112 | tf_op jit(solution)/shard_map/all_to_all | solution.py:398
  18.6 3.2 %collective-permute-start.3 = (bf16[8,208,128]{2,1,0:T(8,128)(2,1)S(1)}, bf16[8,208,128]{2,1,0:T(8,128)(2,1)S(1)}, u32[]{:S(2)}, u32[]{:S(2)}) collective-permute-start(bf16[8,208,128]{2,1,0:T(8,128)(2,1)S(1)} %slice.39), channel_id=1, source_target_pairs={{0,1},{1,0},{2,3},{3,2},{4,5},{5,4},{6,7},{7,6},{8,9},{9,8},{10,11... | collective-permute-start | bytes 1277960 | tf_op jit(solution)/shard_map/ppermute | solution.py:401
  18.8 8.9 %collective-permute-start.2 = (bf16[272,128]{1,0:T(8,128)(2,1)S(1)}, bf16[272,128]{1,0:T(8,128)(2,1)S(1)}, u32[]{:S(2)}, u32[]{:S(2)}) collective-permute-start(bf16[272,128]{1,0:T(8,128)(2,1)S(1)} %fusion.4), channel_id=1, source_target_pairs={{0,16},{16,0},{1,17},{17,1},{2,18},{18,2},{3,19},{19,3},{4,20},{20... | collective-permute-start | bytes 208904 | tf_op jit(solution)/shard_map/ppermute | solution.py:404
  21.5 7.3 %collective-permute-start = (bf16[272,128]{1,0:T(8,128)(2,1)S(1)}, bf16[272,128]{1,0:T(8,128)(2,1)S(1)}, u32[]{:S(2)}, u32[]{:S(2)}) collective-permute-start(bf16[272,128]{1,0:T(8,128)(2,1)S(1)} %fusion.3), channel_id=1, source_target_pairs={{0,16},{16,0},{1,17},{17,1},{2,18},{18,2},{3,19},{19,3},{4,20},{20... | collective-permute-start | bytes 208904 | tf_op jit(solution)/shard_map/ppermute | solution.py:404
  27.7 1.3 %collective-permute-start.4 = (bf16[272,128]{1,0:T(8,128)(2,1)S(1)}, bf16[272,128]{1,0:T(8,128)(2,1)S(1)}, u32[]{:S(2)}, u32[]{:S(2)}) collective-permute-start(bf16[272,128]{1,0:T(8,128)(2,1)S(1)} %collective-permute-done.2.refs_0_.refs_2_), channel_id=1, source_target_pairs={{0,1},{1,0},{2,3},{3,2},{4,5},{5,4},{6,7},{7,6},{8,9},{9,8},{10,11... | collective-permute-start | bytes 208904 | tf_op jit(solution)/shard_map/ppermute | solution.py:401
  28.8 1.3 %collective-permute-start.1 = (bf16[272,128]{1,0:T(8,128)(2,1)S(1)}, bf16[272,128]{1,0:T(8,128)(2,1)S(1)}, u32[]{:S(2)}, u32[]{:S(2)}) collective-permute-start(bf16[272,128]{1,0:T(8,128)(2,1)S(1)} %collective-permute-done.refs_0_), channel_id=1, source_target_pairs={{0,1},{1,0},{2,3},{3,2},{4,5},{5,4},{6,7},{7,6},{8,9},{9,8},{10,11... | collective-permute-start | bytes 208904 | tf_op jit(solution)/shard_map/ppermute | solution.py:401
  30.7 1.2 %collective-permute-start.5 = (f32[8,128]{1,0:T(8,128)S(1)}, f32[8,128]{1,0:T(8,128)S(1)}, u32[]{:S(2)}, u32[]{:S(2)}) collective-permute-start(f32[8,128]{1,0:T(8,128)S(1)} %get-tuple-element.59), channel_id=1, source_target_pairs={{0,1},{1,0},{2,3},{3,2},{4,5},{5,4},{6,7},{7,6},{8,9},{9,8},{10,11... | collective-permute-start | bytes 12296 | tf_op jit(solution)/shard_map/ppermute | solution.py:401
  31.9 4.7 %collective-permute-start.7 = (bf16[8,192,128]{2,1,0:T(8,128)(2,1)S(1)}, bf16[8,192,128]{2,1,0:T(8,128)(2,1)S(1)}, u32[]{:S(2)}, u32[]{:S(2)}) collective-permute-start(bf16[8,192,128]{2,1,0:T(8,128)(2,1)S(1)} %get-tuple-element.67), channel_id=1, source_target_pairs={{0,1},{1,0},{2,3},{3,2},{4,5},{5,4},{6,7},{7,6},{8,9},{9,8},{10,11... | collective-permute-start | bytes 1179656 | tf_op jit(solution)/shard_map/ppermute | solution.py:401
  32.1 4.5 %collective-permute-start.6 = (f32[16,128]{1,0:T(8,128)S(1)}, f32[16,128]{1,0:T(8,128)S(1)}, u32[]{:S(2)}, u32[]{:S(2)}) collective-permute-start(f32[16,128]{1,0:T(8,128)S(1)} %pad_maximum_fusion), channel_id=1, source_target_pairs={{0,16},{16,0},{1,17},{17,1},{2,18},{18,2},{3,19},{19,3},{4,20},{20... | collective-permute-start | bytes 24584 | tf_op jit(solution)/shard_map/ppermute | solution.py:404

commit v3 on v2

--- a/solution.py
+++ b/solution.py
@@ -206,7 +206,8 @@
                     at = pl.ds(((p * per + j) * G + g) * rows, rows)
                     kx[at] = ref[2 * j * rows:(2 * j + 1) * rows]
                     vx[at] = ref[(2 * j + 1) * rows:(2 * j + 2) * rows]
-                    dx[at] = sel[:rows] * ref[2 * per * rows:2 * per * rows + DOC_ROWS][j:j + 1]
+                    source = (TILES - len(parts) + p) * per + j
+                    dx[at] = sel[:rows] * parts[-1][g][2 * per * rows:2 * per * rows + DOC_ROWS][source:source + 1]
         keys_x, values_x = kx[...], vx[...]
         kxt, vxt = dot_nt(eye, keys_x).astype(bf16), dot_nt(eye, values_x).astype(bf16)
         sx = jnp.where(doc_cols(dx[...]) == stats[2:3, mine], dot_nt(keys_x, qt), MASKED)
@@ -296,9 +297,9 @@
     def body(g, slot):
         for u in range(TILES):
             x0 = u * per * rows
-            pair = (query_refs[u * G + g], query_refs[u * G + (g ^ (G // 2))])
+            pair = (query_refs[G + g], query_refs[G + (g ^ (G // 2))])
             dq = jnp.concatenate([sel * ref[2 * per * rows:2 * per * rows + DOC_ROWS][j:j + 1]
-                                  for j in range(per) for ref in pair], 0)
+                                  for j in range(u * per, (u + 1) * per) for ref in pair], 0)
             qdoc = dot_nt(jnp.ones((16, HD), jnp.bfloat16), dq)[0:1]
             s = dot_nt(keys[x0:], far_rows(query_refs, g, G, u, rows, 0)) * (SCALE * LOG2E)
             products[2 * u][slot] = jnp.where(docs[x0:] == qdoc, s, MASKED)
@@ -408,12 +409,9 @@
     sent_across = jnp.where(lax.axis_index("half") == 0, own[:, 6 * rows:8 * rows], queries_here)
     per = H // TILES
 
-    def part_across(u):
-        at = slice(u * per, (u + 1) * per)
-        docs = jnp.pad(own[at, 8 * rows], ((0, DOC_ROWS - per), (0, 0)))
-        return across(jnp.concatenate([sent_across[at].reshape(-1, HD), docs], 0))
-
-    upper, lower = part_across(1), part_across(0)
+    docs = jnp.pad(own[:, 8 * rows], ((0, DOC_ROWS - H), (0, 0)))
+    upper = across(jnp.concatenate([sent_across[per:].reshape(-1, HD), docs], 0))
+    lower = across(sent_across[:per].reshape(-1, HD))
     swaps = [to_member(own[:, (2 if g == G // 2 else 4) * rows:], g) for g in range(1, G)]
     nd, lanes = tile_sizes(rows, G)
     nq = TILES * lanes

time: 50.4 us -> 50.4 us (level)
  no operation moved by 1% of the time
where the time goes in v3:
time: 50.4 us; the launch traced here: 50.1 us
  waiting for transfers between devices  19.5 us (39%)
  blocking collectives  12 us (24%)
  starting transfers between devices  10.3 us (20%)
  Pallas kernels  7.39 us (15%)
  between operations  0.73 us (1%)
    all_to_all x1, blocking collectives, to_head(): return lax.all_to_all(x, 'head', 0, 0, tiled=True)  12 us
    all_to_all x1, waiting for transfers between devices, to_head(): return lax.all_to_all(x, 'head', 0, 0, tiled=True)  9.42 us
    ppermute x3, waiting for transfers between devices, across(): return lax.ppermute(x, 'half', [(0, 1), (1, 0)])  8.61 us
    all_to_all x1, starting transfers between devices, to_head(): return lax.all_to_all(x, 'head', 0, 0, tiled=True)  6.2 us
    ppermute x3, starting transfers between devices, across(): return lax.ppermute(x, 'half', [(0, 1), (1, 0)])  3.68 us
    pallas_call x1, Pallas kernels, per_device(): call(functools.partial(pack_kernel, r0, rows, G), shape(message, bf16), [...  2.35 us
    pallas_call x1, Pallas kernels, per_device(): call(functools.partial(local_kernel, r0, rows, G), [shape((n, HD), bf16)]...  1.65 us
    ppermute x5, waiting for transfers between devices, to_member(): return lax.ppermute(x, 'member', [(i, i ^ g) for i in range(G)])  1.51 us
  transfers between devices with their start and end apart: 9, of which 7 were waited for; matrix products, arithmetic and copies ran while one was open for 0% of the time, Pallas kernels for 6%

profile of v3, /device:TPU:0, one launch (start us, length us, event | category | flops | bytes accessed | tf_op | source)
XLA Modules:
  0.0 50.1 jit_solution(9550633872500771378)
XLA Ops:
  0.6 2.3 %shard_map.84 = bf16[8,272,128]{2,1,0:T(8,128)(2,1)} custom-call(bf16[128,1024]{1,0:T(8,128)(2,1)} %q_in.1, bf16[128,1024]{1,0:T(8,128)(2,1)} %k_in.1, bf16[128,1024]{1,0:T(8,128)(2,1)} %v_in.1, bf16[128,1024]{1,0:T(8,128)(2,1)} %g_in.1, s32[1,128]{1,0:T(1,128)} %bitcast.9), custom_call_target="tpu_custom_call" | custom-call | tf_op jit(solution)/shard_map/pallas_call | solution.py:392
  3.0 6.2 %all-to-all-start = ((bf16[8,272,128]{2,1,0:T(8,128)(2,1)}), bf16[8,272,128]{2,1,0:T(8,128)(2,1)S(1)}, u32[]{:S(2)}, u32[]{:S(2)}) async-start(bf16[8,272,128]{2,1,0:T(8,128)(2,1)} %shard_map.84), calls=%async_computation | async-start | bytes 1114112 | tf_op jit(solution)/shard_map/all_to_all | solution.py:399
  9.2 9.4 %all-to-all-done.refs_0_.own_ref = bf16[8,272,128]{2,1,0:T(8,128)(2,1)S(1)} async-done(((bf16[8,272,128]{2,1,0:T(8,128)(2,1)}), bf16[8,272,128]{2,1,0:T(8,128)(2,1)S(1)}, u32[]{:S(2)}, u32[]{:S(2)}) %all-to-all-start) | async-done | bytes 557088 | tf_op jit(solution)/shard_map/all_to_all | solution.py:399
  18.6 0.1 collective-permute-start.3
  18.8 2.7 %collective-permute-start.2 = (bf16[272,128]{1,0:T(8,128)(2,1)S(1)}, bf16[272,128]{1,0:T(8,128)(2,1)S(1)}, u32[]{:S(2)}, u32[]{:S(2)}) collective-permute-start(bf16[272,128]{1,0:T(8,128)(2,1)S(1)} %fusion.2), channel_id=1, source_target_pairs={{0,16},{16,0},{1,17},{17,1},{2,18},{18,2},{3,19},{19,3},{4,20},{20... | collective-permute-start | bytes 208904 | tf_op jit(solution)/shard_map/ppermute | solution.py:405
  21.5 0.3 collective-permute-start
  21.8 1.7 %shard_map.85 = (bf16[512,128]{1,0:T(8,128)(2,1)S(1)}, bf16[512,128]{1,0:T(8,128)(2,1)S(1)}, bf16[512,128]{1,0:T(8,128)(2,1)S(1)}, bf16[512,128]{1,0:T(8,128)(2,...) custom-call(bf16[8,272,128]{2,1,0:T(8,128)(2,1)S(1)} %all-to-all-don, ...), custom_call_target="tpu_custom_call" | custom-call | tf_op jit(solution)/shard_map/pallas_call | solution.py:420
  23.5 4.2 %collective-permute-done.2.refs_0_.refs_2_ = bf16[272,128]{1,0:T(8,128)(2,1)S(1)} collective-permute-done((bf16[272,128]{1,0:T(8,128)(2,1)S(1)}, bf16[272,128]{1,0:T(8,128)(2,1)S(1)}, u32[]{:S(2)}, u32[]{:S(2)}) %collective-permute-start.2) | collective-permute-done | bytes 69664 | tf_op jit(solution)/shard_map/ppermute | solution.py:405
  27.6 0.0 collective-permute-start.4
  27.7 1.0 %collective-permute-done.refs_0_ = bf16[256,128]{1,0:T(8,128)(2,1)S(1)} collective-permute-done((bf16[256,128]{1,0:T(8,128)(2,1)S(1)}, bf16[256,128]{1,0:T(8,128)(2,1)S(1)}, u32[]{:S(2)}, u32[]{:S(2)}) %collective-permute-start) | collective-permute-done | bytes 65568 | tf_op jit(solution)/shard_map/ppermute | solution.py:405
  28.6 0.0 collective-permute-start.1
  28.7 0.3 collective-permute-done.4.refs_1_.refs_3_
  28.9 0.7 %shard_map.86 = (f32[8,128]{1,0:T(8,128)S(1)}, bf16[256,128]{1,0:T(8,128)(2,1)S(1)}, bf16[256,128]{1,0:T(8,128)(2,1)S(1)}, f32[512,128]{1,0:T(8,128)S(1)}, f32[5...) custom-call(bf16[272,128]{1,0:T(8,128)(2,1)S(1)} %collective-permute-done.2.refs_0_.refs_2_, ...), custom_call_target="tpu_custom_call" | custom-call | tf_op jit(solution)/shard_map/pallas_call | solution.py:431
  29.7 0.2 collective-permute-done.1.refs_1_
  29.9 0.6 %shard_map.87 = (f32[8,128]{1,0:T(8,128)S(1)}, bf16[8,64,128]{2,1,0:T(8,128)(2,1)S(1)}, f32[8,128,128]{2,1,0:T(8,128)S(1)}, bf16[8,192,128]{2,1,0:T(8,128)(2,1)S(1)}) custom-call(bf16[256,128]{1,0:T(8,128)(2,1)S(1)} %collective-permute-done.refs_0_, bf16[256,128]{1,0:T(8,128)(2,1)S(1)} %collective-permute-done.1.refs_1_, ...), custom_call_target="tpu_custom_call" | custom-call | tf_op jit(solution)/shard_map/pallas_call | solution.py:438
  30.5 0.2 collective-permute-start.5
  30.7 1.0 %collective-permute-done.5 = f32[8,128]{1,0:T(8,128)S(1)} collective-permute-done((f32[8,128]{1,0:T(8,128)S(1)}, f32[8,128]{1,0:T(8,128)S(1)}, u32[]{:S(2)}, u32[]{:S(2)}) %collective-permute-start.5) | collective-permute-done | bytes 4128 | tf_op jit(solution)/shard_map/ppermute | solution.py:402
  31.7 0.2 collective-permute-start.7
  31.9 0.7 %collective-permute-start.6 = (f32[16,128]{1,0:T(8,128)S(1)}, f32[16,128]{1,0:T(8,128)S(1)}, u32[]{:S(2)}, u32[]{:S(2)}) collective-permute-start(f32[16,128]{1,0:T(8,128)S(1)} %pad_maximum_fusion), channel_id=1, source_target_pairs={{0,16},{16,0},{1,17},{17,1},{2,18},{18,2},{3,19},{19,3},{4,20},{20... | collective-permute-start | bytes 24584 | tf_op jit(solution)/shard_map/ppermute | solution.py:405
  32.6 0.4 shard_map.88
  33.0 3.4 %collective-permute-done.6.refs_4_ = f32[16,128]{1,0:T(8,128)S(1)} collective-permute-done((f32[16,128]{1,0:T(8,128)S(1)}, f32[16,128]{1,0:T(8,128)S(1)}, u32[]{:S(2)}, u32[]{:S(2)}) %collective-permute-start.6) | collective-permute-done | bytes 8224 | tf_op jit(solution)/shard_map/ppermute | solution.py:405
  36.4 0.4 shard_map.89
  36.8 12.0 %all_to_all.10.in_ref = bf16[8,256,128]{2,1,0:T(8,128)(2,1)S(1)} all-to-all(bf16[8,256,128]{2,1,0:T(8,128)(2,1)S(1)} %shard_map.89), channel_id=1, replica_groups=mesh['half'=2,'head'=8,'member'=2,'dp'=1] {'head'}, dimensions={0} | all-to-all | bytes 1048576 | tf_op jit(solution)/shard_map/all_to_all | solution.py:399
  48.8 1.3 %shard_map.90 = (bf16[128,1024]{1,0:T(8,128)(2,1)}, bf16[128,1024]{1,0:T(8,128)(2,1)}, bf16[128,1024]{1,0:T(8,128)(2,1)}, bf16[128,1024]{1,0:T(8,128)(2,1)}) custom-call(bf16[8,256,128]{2,1,0:T(8,128)(2,1)S(1)} %all_to_all.10.in_ref), custom_call_target="tpu_custom_call" | custom-call | tf_op jit(solution)/shard_map/pallas_call | solution.py:458
  (9 shorter events, 0.1 us)
Async XLA Ops:
  3.0 15.6 %all-to-all-start = ((bf16[8,272,128]{2,1,0:T(8,128)(2,1)}), bf16[8,272,128]{2,1,0:T(8,128)(2,1)S(1)}, u32[]{:S(2)}, u32[]{:S(2)}) async-start(bf16[8,272,128]{2,1,0:T(8,128)(2,1)} %shard_map.84), calls=%async_computation | async-start | bytes 1114112 | tf_op jit(solution)/shard_map/all_to_all | solution.py:399
  18.6 3.2 %collective-permute-start.3 = (bf16[8,208,128]{2,1,0:T(8,128)(2,1)S(1)}, bf16[8,208,128]{2,1,0:T(8,128)(2,1)S(1)}, u32[]{:S(2)}, u32[]{:S(2)}) collective-permute-start(bf16[8,208,128]{2,1,0:T(8,128)(2,1)S(1)} %slice.34), channel_id=1, source_target_pairs={{0,1},{1,0},{2,3},{3,2},{4,5},{5,4},{6,7},{7,6},{8,9},{9,8},{10,11... | collective-permute-start | bytes 1277960 | tf_op jit(solution)/shard_map/ppermute | solution.py:402
  18.8 8.8 %collective-permute-start.2 = (bf16[272,128]{1,0:T(8,128)(2,1)S(1)}, bf16[272,128]{1,0:T(8,128)(2,1)S(1)}, u32[]{:S(2)}, u32[]{:S(2)}) collective-permute-start(bf16[272,128]{1,0:T(8,128)(2,1)S(1)} %fusion.2), channel_id=1, source_target_pairs={{0,16},{16,0},{1,17},{17,1},{2,18},{18,2},{3,19},{19,3},{4,20},{20... | collective-permute-start | bytes 208904 | tf_op jit(solution)/shard_map/ppermute | solution.py:405
  21.5 7.2 %collective-permute-start = (bf16[256,128]{1,0:T(8,128)(2,1)S(1)}, bf16[256,128]{1,0:T(8,128)(2,1)S(1)}, u32[]{:S(2)}, u32[]{:S(2)}) collective-permute-start(bf16[256,128]{1,0:T(8,128)(2,1)S(1)} %bitcast.7), channel_id=1, source_target_pairs={{0,16},{16,0},{1,17},{17,1},{2,18},{18,2},{3,19},{19,3},{4,20},{20... | collective-permute-start | bytes 196616 | tf_op jit(solution)/shard_map/ppermute | solution.py:405
  27.6 1.3 %collective-permute-start.4 = (bf16[272,128]{1,0:T(8,128)(2,1)S(1)}, bf16[272,128]{1,0:T(8,128)(2,1)S(1)}, u32[]{:S(2)}, u32[]{:S(2)}) collective-permute-start(bf16[272,128]{1,0:T(8,128)(2,1)S(1)} %collective-permute-done.2.refs_0_.refs_2_), channel_id=1, source_target_pairs={{0,1},{1,0},{2,3},{3,2},{4,5},{5,4},{6,7},{7,6},{8,9},{9,8},{10,11... | collective-permute-start | bytes 208904 | tf_op jit(solution)/shard_map/ppermute | solution.py:402
  28.6 1.3 %collective-permute-start.1 = (bf16[256,128]{1,0:T(8,128)(2,1)S(1)}, bf16[256,128]{1,0:T(8,128)(2,1)S(1)}, u32[]{:S(2)}, u32[]{:S(2)}) collective-permute-start(bf16[256,128]{1,0:T(8,128)(2,1)S(1)} %collective-permute-done.refs_0_), channel_id=1, source_target_pairs={{0,1},{1,0},{2,3},{3,2},{4,5},{5,4},{6,7},{7,6},{8,9},{9,8},{10,11... | collective-permute-start | bytes 196616 | tf_op jit(solution)/shard_map/ppermute | solution.py:402
  30.5 1.2 %collective-permute-start.5 = (f32[8,128]{1,0:T(8,128)S(1)}, f32[8,128]{1,0:T(8,128)S(1)}, u32[]{:S(2)}, u32[]{:S(2)}) collective-permute-start(f32[8,128]{1,0:T(8,128)S(1)} %get-tuple-element.59), channel_id=1, source_target_pairs={{0,1},{1,0},{2,3},{3,2},{4,5},{5,4},{6,7},{7,6},{8,9},{9,8},{10,11... | collective-permute-start | bytes 12296 | tf_op jit(solution)/shard_map/ppermute | solution.py:402
  31.7 4.7 %collective-permute-start.7 = (bf16[8,192,128]{2,1,0:T(8,128)(2,1)S(1)}, bf16[8,192,128]{2,1,0:T(8,128)(2,1)S(1)}, u32[]{:S(2)}, u32[]{:S(2)}) collective-permute-start(bf16[8,192,128]{2,1,0:T(8,128)(2,1)S(1)} %get-tuple-element.67), channel_id=1, source_target_pairs={{0,1},{1,0},{2,3},{3,2},{4,5},{5,4},{6,7},{7,6},{8,9},{9,8},{10,11... | collective-permute-start | bytes 1179656 | tf_op jit(solution)/shard_map/ppermute | solution.py:402
  31.9 4.5 %collective-permute-start.6 = (f32[16,128]{1,0:T(8,128)S(1)}, f32[16,128]{1,0:T(8,128)S(1)}, u32[]{:S(2)}, u32[]{:S(2)}) collective-permute-start(f32[16,128]{1,0:T(8,128)S(1)} %pad_maximum_fusion), channel_id=1, source_target_pairs={{0,16},{16,0},{1,17},{17,1},{2,18},{18,2},{3,19},{19,3},{4,20},{20... | collective-permute-start | bytes 24584 | tf_op jit(solution)/shard_map/ppermute | solution.py:405

commit v4 on v3

--- a/solution.py
+++ b/solution.py
@@ -177,18 +177,17 @@
         dp_refs[2 * u][...], dp_refs[2 * u + 1][...] = dot_nt(v1[0:nk], gt), dot_nt(v2[0:nk], gt)
 
 
-def finish_tile(u, r0, rows, members, parts, shared, products, results, scratch):
+def finish_tile(u, r0, rows, members, parts, shared, products, results):
     far = (lax.axis_index("half") == 1) & jnp.logical_not(takes_fine(members))
     for branch, with_far in ((far, True), (jnp.logical_not(far), False)):
         pl.when(branch)(functools.partial(
-            tile_body, u, r0, rows, members, with_far, parts, shared, products, results, scratch))
-
-
-def tile_body(u, r0, rows, members, with_far, parts, shared, products, results, scratch):
+            tile_body, u, r0, rows, members, with_far, parts, shared, products, results))
+
+
+def tile_body(u, r0, rows, members, with_far, parts, shared, products, results):
     G = members
     q_all, g_all, stats, local_out, gtt_ref, k1, k2 = shared
     far_stats, att, gq_ref, sums = results[0], results[1], results[2], results[3:]
-    kx, vx, dx = scratch
     bf16 = jnp.bfloat16
     per = H // TILES
     eye = eye_matrix()
@@ -200,17 +199,14 @@
     top, total, out = stats[0:1, mine], stats[1:2, mine], local_out[:, mine]
     if with_far:
         sel = selector(lax.axis_index("head"), r0, rows, HD, False)
-        for p, part in enumerate(parts):
-            for j in range(per):
-                for g, ref in enumerate(part):
-                    at = pl.ds(((p * per + j) * G + g) * rows, rows)
-                    kx[at] = ref[2 * j * rows:(2 * j + 1) * rows]
-                    vx[at] = ref[(2 * j + 1) * rows:(2 * j + 2) * rows]
-                    source = (TILES - len(parts) + p) * per + j
-                    dx[at] = sel[:rows] * parts[-1][g][2 * per * rows:2 * per * rows + DOC_ROWS][source:source + 1]
-        keys_x, values_x = kx[...], vx[...]
+        size = per * rows
+        keys_x, values_x = (jnp.concatenate([ref[lo:lo + size] for part in parts for ref in part], 0) for lo in (0, size))
+        first = TILES - len(parts)
+        docs_x = jnp.concatenate([sel[:rows] * ref[2 * size:2 * size + DOC_ROWS][source:source + 1]
+                                  for p in range(first, TILES) for ref in parts[-1]
+                                  for source in range(p * per, (p + 1) * per)], 0)
         kxt, vxt = dot_nt(eye, keys_x).astype(bf16), dot_nt(eye, values_x).astype(bf16)
-        sx = jnp.where(doc_cols(dx[...]) == stats[2:3, mine], dot_nt(keys_x, qt), MASKED)
+        sx = jnp.where(doc_cols(docs_x) == stats[2:3, mine], dot_nt(keys_x, qt), MASKED)
         local_top = top
         top = jnp.maximum(local_top, jnp.max(sx, 0, keepdims=True))
         px = jnp.exp2(sx * c - top * c)
@@ -244,7 +240,7 @@
 
 def last_tile_kernel(r0, rows, members, *refs):
     G = members
-    finish_tile(1, r0, rows, G, [refs[:G]], refs[G:G + 7], refs[G + 7:G + 11], refs[G + 11:G + 18], refs[G + 18:])
+    finish_tile(1, r0, rows, G, [refs[:G]], refs[G:G + 7], refs[G + 7:G + 11], refs[G + 11:G + 18])
 
 
 def first_tile_kernel(r0, rows, members, *refs):
@@ -255,7 +251,7 @@
     nd, lanes = tile_sizes(rows, G)
     first = (far_stats,) + tuple(scratch[:6])
     far_stats[...] = last[0][...]
-    finish_tile(0, r0, rows, G, parts, shared, products, first, scratch[6:])
+    finish_tile(0, r0, rows, G, parts, shared, products, first)
     partner, per = G // 2, H // TILES
     for j in range(H):
         att, gq = (first, last)[j // per][1:3]
@@ -273,8 +269,9 @@
 
 
 def far_rows(query_refs, g, members, u, rows, lo):
+    size = H // TILES * rows
     pair = (query_refs[u * members + g], query_refs[u * members + (g ^ (members // 2))])
-    return jnp.concatenate([ref[(2 * j + lo) * rows:(2 * j + lo + 1) * rows] for j in range(H // TILES) for ref in pair], 0)
+    return jnp.concatenate([ref[at:at + rows] for at in range(lo * size, (lo + 1) * size, rows) for ref in pair], 0)
 
 
 def far_slots(members, body):
@@ -410,8 +407,11 @@
     per = H // TILES
 
     docs = jnp.pad(own[:, 8 * rows], ((0, DOC_ROWS - H), (0, 0)))
-    upper = across(jnp.concatenate([sent_across[per:].reshape(-1, HD), docs], 0))
-    lower = across(sent_across[:per].reshape(-1, HD))
+    def part(at):
+        return [sent_across[at, lo * rows:(lo + 1) * rows].reshape(-1, HD) for lo in range(2)]
+
+    upper = across(jnp.concatenate(part(slice(per, H)) + [docs], 0))
+    lower = across(jnp.concatenate(part(slice(0, per)), 0))
     swaps = [to_member(own[:, (2 if g == G // 2 else 4) * rows:], g) for g in range(1, G)]
     nd, lanes = tile_sizes(rows, G)
     nq = TILES * lanes
@@ -427,11 +427,10 @@
     upper, k1 = lax.optimization_barrier((upper, k1))
     uppers = [upper] + [to_member(upper, g) for g in range(1, G)]
     tile_rows = pltpu.VMEM((lanes, HD), bf16)
-    far_scratch = lambda keys: [pltpu.VMEM((keys, HD), bf16)] * 3
     last = call(
         functools.partial(last_tile_kernel, r0, rows, G),
         [shape((8, HD), f32)] + [shape((lanes, HD), bf16)] * 2 + [shape((n, HD), f32)] * 4,
-        far_scratch(nd), limit=32,
+        limit=32,
     )(*uppers, *shared, *products[2:4], *products[6:8])
     lowers = [lower] + [to_member(lower, g) for g in range(1, G)]
     sent = lambda g: (H, (6 if g == G // 2 else 4) * rows, HD)
@@ -439,7 +438,7 @@
         functools.partial(first_tile_kernel, r0, rows, G),
         [shape((8, HD), f32), shape((H, 2 * rows, HD), bf16), shape((H, 4 * rows, HD), f32)]
         + [shape(sent(g), bf16) for g in range(1, G)],
-        [tile_rows] * 2 + [pltpu.VMEM((nd, HD), f32)] * 4 + far_scratch(n), limit=32,
+        [tile_rows] * 2 + [pltpu.VMEM((nd, HD), f32)] * 4, limit=32,
     )(*lowers, *uppers, *shared, *products[0:2], *products[4:6], *last)
     crosses = lowers + uppers
     hops = [to_member(outs[0], g) for g in range(1, G)]

time: 50.4 us -> 50.3 us (level)
  no operation moved by 1% of the time
where the time goes in v4:
time: 50.3 us; the launch traced here: 50.1 us
  waiting for transfers between devices  19.6 us (39%)
  blocking collectives  12 us (24%)
  starting transfers between devices  10.3 us (20%)
  Pallas kernels  7.38 us (15%)
  between operations  0.73 us (1%)
    all_to_all x1, blocking collectives, to_head(): return lax.all_to_all(x, 'head', 0, 0, tiled=True)  12 us
    all_to_all x1, waiting for transfers between devices, to_head(): return lax.all_to_all(x, 'head', 0, 0, tiled=True)  9.42 us
    ppermute x3, waiting for transfers between devices, across(): return lax.ppermute(x, 'half', [(0, 1), (1, 0)])  8.63 us
    all_to_all x1, starting transfers between devices, to_head(): return lax.all_to_all(x, 'head', 0, 0, tiled=True)  6.2 us
    ppermute x3, starting transfers between devices, across(): return lax.ppermute(x, 'half', [(0, 1), (1, 0)])  3.66 us
    pallas_call x1, Pallas kernels, per_device(): call(functools.partial(pack_kernel, r0, rows, G), shape(message, bf16), [...  2.35 us
    pallas_call x1, Pallas kernels, per_device(): call(functools.partial(local_kernel, r0, rows, G), [shape((n, HD), bf16)]...  1.64 us
    ppermute x5, waiting for transfers between devices, to_member(): return lax.ppermute(x, 'member', [(i, i ^ g) for i in range(G)])  1.51 us
  transfers between devices with their start and end apart: 9, of which 7 were waited for; matrix products, arithmetic and copies ran while one was open for 0% of the time, Pallas kernels for 6%

profile of v4, /device:TPU:0, one launch (start us, length us, event | category | flops | bytes accessed | tf_op | source)
XLA Modules:
  0.0 50.1 jit_solution(10971835813487203273)
XLA Ops:
  0.6 2.3 %shard_map.84 = bf16[8,272,128]{2,1,0:T(8,128)(2,1)} custom-call(bf16[128,1024]{1,0:T(8,128)(2,1)} %q_in.1, bf16[128,1024]{1,0:T(8,128)(2,1)} %k_in.1, bf16[128,1024]{1,0:T(8,128)(2,1)} %v_in.1, bf16[128,1024]{1,0:T(8,128)(2,1)} %g_in.1, s32[1,128]{1,0:T(1,128)} %bitcast.13), custom_call_target="tpu_custom_call" | custom-call | tf_op jit(solution)/shard_map/pallas_call | solution.py:389
  3.0 6.2 %all-to-all-start = ((bf16[8,272,128]{2,1,0:T(8,128)(2,1)}), bf16[8,272,128]{2,1,0:T(8,128)(2,1)S(1)}, u32[]{:S(2)}, u32[]{:S(2)}) async-start(bf16[8,272,128]{2,1,0:T(8,128)(2,1)} %shard_map.84), calls=%async_computation | async-start | bytes 1114112 | tf_op jit(solution)/shard_map/all_to_all | solution.py:396
  9.2 9.4 %all-to-all-done.refs_0_.own_ref = bf16[8,272,128]{2,1,0:T(8,128)(2,1)S(1)} async-done(((bf16[8,272,128]{2,1,0:T(8,128)(2,1)}), bf16[8,272,128]{2,1,0:T(8,128)(2,1)S(1)}, u32[]{:S(2)}, u32[]{:S(2)}) %all-to-all-start) | async-done | bytes 557088 | tf_op jit(solution)/shard_map/all_to_all | solution.py:396
  18.6 0.1 collective-permute-start.3
  18.8 2.7 %collective-permute-start.2 = (bf16[272,128]{1,0:T(8,128)(2,1)S(1)}, bf16[272,128]{1,0:T(8,128)(2,1)S(1)}, u32[]{:S(2)}, u32[]{:S(2)}) collective-permute-start(bf16[272,128]{1,0:T(8,128)(2,1)S(1)} %fusion.2), channel_id=1, source_target_pairs={{0,16},{16,0},{1,17},{17,1},{2,18},{18,2},{3,19},{19,3},{4,20},{20... | collective-permute-start | bytes 208904 | tf_op jit(solution)/shard_map/ppermute | solution.py:402
  21.5 0.3 collective-permute-start
  21.8 0.0 collective-permute-done.3.refs_1_
  21.8 1.6 %shard_map.85 = (bf16[512,128]{1,0:T(8,128)(2,1)S(1)}, bf16[512,128]{1,0:T(8,128)(2,1)S(1)}, bf16[512,128]{1,0:T(8,128)(2,1)S(1)}, bf16[512,128]{1,0:T(8,128)(2,...) custom-call(bf16[8,272,128]{2,1,0:T(8,128)(2,1)S(1)} %all-to-all-don, ...), custom_call_target="tpu_custom_call" | custom-call | tf_op jit(solution)/shard_map/pallas_call | solution.py:420
  23.5 4.2 %collective-permute-done.2.refs_0_.refs_2_ = bf16[272,128]{1,0:T(8,128)(2,1)S(1)} collective-permute-done((bf16[272,128]{1,0:T(8,128)(2,1)S(1)}, bf16[272,128]{1,0:T(8,128)(2,1)S(1)}, u32[]{:S(2)}, u32[]{:S(2)}) %collective-permute-start.2) | collective-permute-done | bytes 69664 | tf_op jit(solution)/shard_map/ppermute | solution.py:402
  27.6 1.0 %collective-permute-done.refs_0_ = bf16[256,128]{1,0:T(8,128)(2,1)S(1)} collective-permute-done((bf16[256,128]{1,0:T(8,128)(2,1)S(1)}, bf16[256,128]{1,0:T(8,128)(2,1)S(1)}, u32[]{:S(2)}, u32[]{:S(2)}) %collective-permute-start) | collective-permute-done | bytes 65568 | tf_op jit(solution)/shard_map/ppermute | solution.py:402
  28.6 0.3 collective-permute-done.4.refs_1_.refs_3_
  28.9 0.7 %shard_map.86 = (f32[8,128]{1,0:T(8,128)S(1)}, bf16[256,128]{1,0:T(8,128)(2,1)S(1)}, bf16[256,128]{1,0:T(8,128)(2,1)S(1)}, f32[512,128]{1,0:T(8,128)S(1)}, f32[5...) custom-call(bf16[272,128]{1,0:T(8,128)(2,1)S(1)} %collective-permute-done.2.refs_0_.refs_2_, ...), custom_call_target="tpu_custom_call" | custom-call | tf_op jit(solution)/shard_map/pallas_call | solution.py:430
  29.7 0.2 collective-permute-done.1.refs_1_
  29.9 0.6 %shard_map.87 = (f32[8,128]{1,0:T(8,128)S(1)}, bf16[8,64,128]{2,1,0:T(8,128)(2,1)S(1)}, f32[8,128,128]{2,1,0:T(8,128)S(1)}, bf16[8,192,128]{2,1,0:T(8,128)(2,1)S(1)}) custom-call(bf16[256,128]{1,0:T(8,128)(2,1)S(1)} %collective-permute-done.refs_0_, bf16[256,128]{1,0:T(8,128)(2,1)S(1)} %collective-permute-done.1.refs_1_, ...), custom_call_target="tpu_custom_call" | custom-call | tf_op jit(solution)/shard_map/pallas_call | solution.py:437
  30.5 0.2 collective-permute-start.5
  30.7 1.0 %collective-permute-done.5 = f32[8,128]{1,0:T(8,128)S(1)} collective-permute-done((f32[8,128]{1,0:T(8,128)S(1)}, f32[8,128]{1,0:T(8,128)S(1)}, u32[]{:S(2)}, u32[]{:S(2)}) %collective-permute-start.5) | collective-permute-done | bytes 4128 | tf_op jit(solution)/shard_map/ppermute | solution.py:399
  31.7 0.2 collective-permute-start.7
  31.9 0.7 %collective-permute-start.6 = (f32[16,128]{1,0:T(8,128)S(1)}, f32[16,128]{1,0:T(8,128)S(1)}, u32[]{:S(2)}, u32[]{:S(2)}) collective-permute-start(f32[16,128]{1,0:T(8,128)S(1)} %pad_maximum_fusion.1), channel_id=1, source_target_pairs={{0,16},{16,0},{1,17},{17,1},{2,18},{18,2},{3,19},{19,3},{4,20},{20... | collective-permute-start | bytes 24584 | tf_op jit(solution)/shard_map/ppermute | solution.py:402
  32.6 0.4 shard_map.88
  33.0 3.4 %collective-permute-done.6.refs_4_ = f32[16,128]{1,0:T(8,128)S(1)} collective-permute-done((f32[16,128]{1,0:T(8,128)S(1)}, f32[16,128]{1,0:T(8,128)S(1)}, u32[]{:S(2)}, u32[]{:S(2)}) %collective-permute-start.6) | collective-permute-done | bytes 8224 | tf_op jit(solution)/shard_map/ppermute | solution.py:402
  36.4 0.0 collective-permute-done.7.refs_11_
  36.4 0.4 shard_map.89
  36.8 12.0 %all_to_all.10.in_ref = bf16[8,256,128]{2,1,0:T(8,128)(2,1)S(1)} all-to-all(bf16[8,256,128]{2,1,0:T(8,128)(2,1)S(1)} %shard_map.89), channel_id=1, replica_groups=mesh['half'=2,'head'=8,'member'=2,'dp'=1] {'head'}, dimensions={0} | all-to-all | bytes 1048576 | tf_op jit(solution)/shard_map/all_to_all | solution.py:396
  48.8 1.3 %shard_map.90 = (bf16[128,1024]{1,0:T(8,128)(2,1)}, bf16[128,1024]{1,0:T(8,128)(2,1)}, bf16[128,1024]{1,0:T(8,128)(2,1)}, bf16[128,1024]{1,0:T(8,128)(2,1)}) custom-call(bf16[8,256,128]{2,1,0:T(8,128)(2,1)S(1)} %all_to_all.10.in_ref), custom_call_target="tpu_custom_call" | custom-call | tf_op jit(solution)/shard_map/pallas_call | solution.py:457
  (10 shorter events, 0.1 us)
Async XLA Ops:
  3.0 15.6 %all-to-all-start = ((bf16[8,272,128]{2,1,0:T(8,128)(2,1)}), bf16[8,272,128]{2,1,0:T(8,128)(2,1)S(1)}, u32[]{:S(2)}, u32[]{:S(2)}) async-start(bf16[8,272,128]{2,1,0:T(8,128)(2,1)} %shard_map.84), calls=%async_computation | async-start | bytes 1114112 | tf_op jit(solution)/shard_map/all_to_all | solution.py:396
  18.6 3.2 %collective-permute-start.3 = (bf16[8,208,128]{2,1,0:T(8,128)(2,1)S(1)}, bf16[8,208,128]{2,1,0:T(8,128)(2,1)S(1)}, u32[]{:S(2)}, u32[]{:S(2)}) collective-permute-start(bf16[8,208,128]{2,1,0:T(8,128)(2,1)S(1)} %slice.44), channel_id=1, source_target_pairs={{0,1},{1,0},{2,3},{3,2},{4,5},{5,4},{6,7},{7,6},{8,9},{9,8},{10,11... | collective-permute-start | bytes 1277960 | tf_op jit(solution)/shard_map/ppermute | solution.py:399
  18.8 8.8 %collective-permute-start.2 = (bf16[272,128]{1,0:T(8,128)(2,1)S(1)}, bf16[272,128]{1,0:T(8,128)(2,1)S(1)}, u32[]{:S(2)}, u32[]{:S(2)}) collective-permute-start(bf16[272,128]{1,0:T(8,128)(2,1)S(1)} %fusion.2), channel_id=1, source_target_pairs={{0,16},{16,0},{1,17},{17,1},{2,18},{18,2},{3,19},{19,3},{4,20},{20... | collective-permute-start | bytes 208904 | tf_op jit(solution)/shard_map/ppermute | solution.py:402
  21.5 7.2 %collective-permute-start = (bf16[256,128]{1,0:T(8,128)(2,1)S(1)}, bf16[256,128]{1,0:T(8,128)(2,1)S(1)}, u32[]{:S(2)}, u32[]{:S(2)}) collective-permute-start(bf16[256,128]{1,0:T(8,128)(2,1)S(1)} %pad_maximum_fusion), channel_id=1, source_target_pairs={{0,16},{16,0},{1,17},{17,1},{2,18},{18,2},{3,19},{19,3},{4,20},{20... | collective-permute-start | bytes 196616 | tf_op jit(solution)/shard_map/ppermute | solution.py:402
  27.6 1.3 %collective-permute-start.4 = (bf16[272,128]{1,0:T(8,128)(2,1)S(1)}, bf16[272,128]{1,0:T(8,128)(2,1)S(1)}, u32[]{:S(2)}, u32[]{:S(2)}) collective-permute-start(bf16[272,128]{1,0:T(8,128)(2,1)S(1)} %collective-permute-done.2.refs_0_.refs_2_), channel_id=1, source_target_pairs={{0,1},{1,0},{2,3},{3,2},{4,5},{5,4},{6,7},{7,6},{8,9},{9,8},{10,11... | collective-permute-start | bytes 208904 | tf_op jit(solution)/shard_map/ppermute | solution.py:399
  28.6 1.3 %collective-permute-start.1 = (bf16[256,128]{1,0:T(8,128)(2,1)S(1)}, bf16[256,128]{1,0:T(8,128)(2,1)S(1)}, u32[]{:S(2)}, u32[]{:S(2)}) collective-permute-start(bf16[256,128]{1,0:T(8,128)(2,1)S(1)} %collective-permute-done.refs_0_), channel_id=1, source_target_pairs={{0,1},{1,0},{2,3},{3,2},{4,5},{5,4},{6,7},{7,6},{8,9},{9,8},{10,11... | collective-permute-start | bytes 196616 | tf_op jit(solution)/shard_map/ppermute | solution.py:399
  30.5 1.2 %collective-permute-start.5 = (f32[8,128]{1,0:T(8,128)S(1)}, f32[8,128]{1,0:T(8,128)S(1)}, u32[]{:S(2)}, u32[]{:S(2)}) collective-permute-start(f32[8,128]{1,0:T(8,128)S(1)} %get-tuple-element.59), channel_id=1, source_target_pairs={{0,1},{1,0},{2,3},{3,2},{4,5},{5,4},{6,7},{7,6},{8,9},{9,8},{10,11... | collective-permute-start | bytes 12296 | tf_op jit(solution)/shard_map/ppermute | solution.py:399
  31.7 4.7 %collective-permute-start.7 = (bf16[8,192,128]{2,1,0:T(8,128)(2,1)S(1)}, bf16[8,192,128]{2,1,0:T(8,128)(2,1)S(1)}, u32[]{:S(2)}, u32[]{:S(2)}) collective-permute-start(bf16[8,192,128]{2,1,0:T(8,128)(2,1)S(1)} %get-tuple-element.67), channel_id=1, source_target_pairs={{0,1},{1,0},{2,3},{3,2},{4,5},{5,4},{6,7},{7,6},{8,9},{9,8},{10,11... | collective-permute-start | bytes 1179656 | tf_op jit(solution)/shard_map/ppermute | solution.py:399
  31.9 4.5 %collective-permute-start.6 = (f32[16,128]{1,0:T(8,128)S(1)}, f32[16,128]{1,0:T(8,128)S(1)}, u32[]{:S(2)}, u32[]{:S(2)}) collective-permute-start(f32[16,128]{1,0:T(8,128)S(1)} %pad_maximum_fusion.1), channel_id=1, source_target_pairs={{0,16},{16,0},{1,17},{17,1},{2,18},{18,2},{3,19},{19,3},{4,20},{20... | collective-permute-start | bytes 24584 | tf_op jit(solution)/shard_map/ppermute | solution.py:402

commit v5 on v4

--- a/solution.py
+++ b/solution.py
@@ -99,8 +99,8 @@
     G = members
     r1 = 2 * r0
     own_ref, swap_refs = refs[0], refs[1:G]
-    (k1, k2, q_all, g_all, stats, out_ref, gtt_ref), rest = refs[G:G + 7], refs[G + 7:]
-    p_refs, dp_refs, (v1, v2, d1, d2) = rest[:2 * TILES], rest[2 * TILES:4 * TILES], rest[4 * TILES:]
+    (k1t, k2t, q_all, g_all, stats, out_ref, gtt_ref), rest = refs[G:G + 7], refs[G + 7:]
+    p_refs, dp_refs, (v1, v2, d1, d2, k1, k2) = rest[:2 * TILES], rest[2 * TILES:4 * TILES], rest[4 * TILES:]
     bf16, f32 = jnp.bfloat16, jnp.float32
     tokens = HD
     head = lax.axis_index("head")
@@ -127,6 +127,7 @@
             d2[at] = sel[rows:] * doc
 
     eye = eye_matrix()
+    k1t[...], k2t[...] = dot_nt(eye, k1[...]).astype(bf16), dot_nt(eye, k2[...]).astype(bf16)
     v1t, v2t = dot_nt(eye, v1[...]).astype(bf16), dot_nt(eye, v2[...]).astype(bf16)
     docs1, docs2 = doc_cols(d1[...]), doc_cols(d2[...])
     nd, lanes = tile_sizes(rows, G)
@@ -232,7 +233,7 @@
     for i, k in enumerate((k1, k2)):
         w = products[i][...] * local_inv
         ds = (w * (products[2 + i][...] - dot)).astype(bf16)
-        gq = gq + dot_nn(dot_nt(eye, k[0:nk]).astype(bf16), ds)
+        gq = gq + dot_nn(k[:, 0:nk], ds)
         sums[i][...] = dot_nn(ds, qt)
         sums[2 + i][...] = dot_nn(w.astype(bf16), gt)
     gq_ref[...] = (gq * SCALE).T.astype(bf16)
@@ -419,9 +420,9 @@
     key_rows = pltpu.VMEM((n, HD), bf16)
     k1, k2, q_all, g_all, stats, out, gtt, *products = call(
         functools.partial(local_kernel, r0, rows, G),
-        [shape((n, HD), bf16)] * 2 + [shape((nq, HD), bf16)] * 2 + [shape((8, nq), f32)]
+        [shape((HD, n), bf16)] * 2 + [shape((nq, HD), bf16)] * 2 + [shape((8, nq), f32)]
         + [shape((HD, nq), f32)] * 2 + tile * 2,
-        [key_rows] * 4, limit=32,
+        [key_rows] * 6, limit=32,
     )(own, *swaps)
     shared = (q_all, g_all, stats, out, gtt, k1, k2)
     upper, k1 = lax.optimization_barrier((upper, k1))

time: 50.3 us -> 50.3 us (level)
  transfers between devices with their start and end apart: 9 -> 9, of which waited for: 7 -> 7; matrix products, arithmetic and copies ran while one was open for 0% -> 0% of each run, Pallas kernels for 6% -> 5%
where the time goes in v5:
time: 50.3 us; the launch traced here: 50 us
  waiting for transfers between devices  19.6 us (39%)
  blocking collectives  12 us (24%)
  starting transfers between devices  10.4 us (21%)
  Pallas kernels  7.2 us (14%)
  between operations  0.73 us (1%)
    all_to_all x1, blocking collectives, to_head(): return lax.all_to_all(x, 'head', 0, 0, tiled=True)  12 us
    all_to_all x1, waiting for transfers between devices, to_head(): return lax.all_to_all(x, 'head', 0, 0, tiled=True)  9.42 us
    ppermute x3, waiting for transfers between devices, across(): return lax.ppermute(x, 'half', [(0, 1), (1, 0)])  8.5 us
    all_to_all x1, starting transfers between devices, to_head(): return lax.all_to_all(x, 'head', 0, 0, tiled=True)  6.2 us
    ppermute x3, starting transfers between devices, across(): return lax.ppermute(x, 'half', [(0, 1), (1, 0)])  3.71 us
    pallas_call x1, Pallas kernels, per_device(): call(functools.partial(pack_kernel, r0, rows, G), shape(message, bf16), [...  2.35 us
    pallas_call x1, Pallas kernels, per_device(): call(functools.partial(local_kernel, r0, rows, G), [shape((HD, n), bf16)]...  1.72 us
    ppermute x5, waiting for transfers between devices, to_member(): return lax.ppermute(x, 'member', [(i, i ^ g) for i in range(G)])  1.69 us
  transfers between devices with their start and end apart: 9, of which 7 were waited for; matrix products, arithmetic and copies ran while one was open for 0% of the time, Pallas kernels for 5%

profile of v5, /device:TPU:0, one launch (start us, length us, event | category | flops | bytes accessed | tf_op | source)
XLA Modules:
  0.0 50.0 jit_solution(1391365856265480703)
XLA Ops:
  0.6 2.3 %shard_map.84 = bf16[8,272,128]{2,1,0:T(8,128)(2,1)} custom-call(bf16[128,1024]{1,0:T(8,128)(2,1)} %q_in.1, bf16[128,1024]{1,0:T(8,128)(2,1)} %k_in.1, bf16[128,1024]{1,0:T(8,128)(2,1)} %v_in.1, bf16[128,1024]{1,0:T(8,128)(2,1)} %g_in.1, s32[1,128]{1,0:T(1,128)} %bitcast.13), custom_call_target="tpu_custom_call" | custom-call | tf_op jit(solution)/shard_map/pallas_call | solution.py:390
  3.0 6.2 %all-to-all-start = ((bf16[8,272,128]{2,1,0:T(8,128)(2,1)}), bf16[8,272,128]{2,1,0:T(8,128)(2,1)S(1)}, u32[]{:S(2)}, u32[]{:S(2)}) async-start(bf16[8,272,128]{2,1,0:T(8,128)(2,1)} %shard_map.84), calls=%async_computation | async-start | bytes 1114112 | tf_op jit(solution)/shard_map/all_to_all | solution.py:397
  9.2 9.4 %all-to-all-done.refs_0_.own_ref = bf16[8,272,128]{2,1,0:T(8,128)(2,1)S(1)} async-done(((bf16[8,272,128]{2,1,0:T(8,128)(2,1)}), bf16[8,272,128]{2,1,0:T(8,128)(2,1)S(1)}, u32[]{:S(2)}, u32[]{:S(2)}) %all-to-all-start) | async-done | bytes 557088 | tf_op jit(solution)/shard_map/all_to_all | solution.py:397
  18.6 0.1 collective-permute-start.3
  18.8 2.7 %collective-permute-start.2 = (bf16[272,128]{1,0:T(8,128)(2,1)S(1)}, bf16[272,128]{1,0:T(8,128)(2,1)S(1)}, u32[]{:S(2)}, u32[]{:S(2)}) collective-permute-start(bf16[272,128]{1,0:T(8,128)(2,1)S(1)} %fusion.2), channel_id=1, source_target_pairs={{0,16},{16,0},{1,17},{17,1},{2,18},{18,2},{3,19},{19,3},{4,20},{20... | collective-permute-start | bytes 208904 | tf_op jit(solution)/shard_map/ppermute | solution.py:403
  21.5 0.3 collective-permute-start
  21.8 0.0 collective-permute-done.3.refs_1_
  21.8 1.7 %shard_map.85 = (bf16[128,512]{1,0:T(8,128)(2,1)S(1)}, bf16[128,512]{1,0:T(8,128)(2,1)S(1)}, bf16[512,128]{1,0:T(8,128)(2,1)S(1)}, bf16[512,128]{1,0:T(8,128)(2,...) custom-call(bf16[8,272,128]{2,1,0:T(8,128)(2,1)S(1)} %all-to-all-don, ...), custom_call_target="tpu_custom_call" | custom-call | tf_op jit(solution)/shard_map/pallas_call | solution.py:421
  23.5 4.1 %collective-permute-done.2.refs_0_.refs_2_ = bf16[272,128]{1,0:T(8,128)(2,1)S(1)} collective-permute-done((bf16[272,128]{1,0:T(8,128)(2,1)S(1)}, bf16[272,128]{1,0:T(8,128)(2,1)S(1)}, u32[]{:S(2)}, u32[]{:S(2)}) %collective-permute-start.2) | collective-permute-done | bytes 69664 | tf_op jit(solution)/shard_map/ppermute | solution.py:403
  27.6 1.0 %collective-permute-done.refs_0_ = bf16[256,128]{1,0:T(8,128)(2,1)S(1)} collective-permute-done((bf16[256,128]{1,0:T(8,128)(2,1)S(1)}, bf16[256,128]{1,0:T(8,128)(2,1)S(1)}, u32[]{:S(2)}, u32[]{:S(2)}) %collective-permute-start) | collective-permute-done | bytes 65568 | tf_op jit(solution)/shard_map/ppermute | solution.py:403
  28.6 0.3 collective-permute-done.4.refs_1_.refs_3_
  28.9 0.6 %shard_map.86 = (f32[8,128]{1,0:T(8,128)S(1)}, bf16[256,128]{1,0:T(8,128)(2,1)S(1)}, bf16[256,128]{1,0:T(8,128)(2,1)S(1)}, f32[512,128]{1,0:T(8,128)S(1)}, f32[5...) custom-call(bf16[272,128]{1,0:T(8,128)(2,1)S(1)} %collective-permute-done.2.refs_0_.refs_2_, ...), custom_call_target="tpu_custom_call" | custom-call | tf_op jit(solution)/shard_map/pallas_call | solution.py:431
  29.5 0.4 collective-permute-done.1.refs_1_
  29.9 0.5 shard_map.87
  30.4 0.2 collective-permute-start.5
  30.6 1.0 %collective-permute-done.5 = f32[8,128]{1,0:T(8,128)S(1)} collective-permute-done((f32[8,128]{1,0:T(8,128)S(1)}, f32[8,128]{1,0:T(8,128)S(1)}, u32[]{:S(2)}, u32[]{:S(2)}) %collective-permute-start.5) | collective-permute-done | bytes 4128 | tf_op jit(solution)/shard_map/ppermute | solution.py:400
  31.6 0.2 collective-permute-start.7
  31.8 0.7 %collective-permute-start.6 = (f32[16,128]{1,0:T(8,128)S(1)}, f32[16,128]{1,0:T(8,128)S(1)}, u32[]{:S(2)}, u32[]{:S(2)}) collective-permute-start(f32[16,128]{1,0:T(8,128)S(1)} %pad_maximum_fusion.1), channel_id=1, source_target_pairs={{0,16},{16,0},{1,17},{17,1},{2,18},{18,2},{3,19},{19,3},{4,20},{20... | collective-permute-start | bytes 24584 | tf_op jit(solution)/shard_map/ppermute | solution.py:403
  32.5 0.4 shard_map.88
  33.0 3.4 %collective-permute-done.6.refs_4_ = f32[16,128]{1,0:T(8,128)S(1)} collective-permute-done((f32[16,128]{1,0:T(8,128)S(1)}, f32[16,128]{1,0:T(8,128)S(1)}, u32[]{:S(2)}, u32[]{:S(2)}) %collective-permute-start.6) | collective-permute-done | bytes 8224 | tf_op jit(solution)/shard_map/ppermute | solution.py:403
  36.4 0.0 collective-permute-done.7.refs_11_
  36.4 0.4 shard_map.89
  36.7 12.0 %all_to_all.10.in_ref = bf16[8,256,128]{2,1,0:T(8,128)(2,1)S(1)} all-to-all(bf16[8,256,128]{2,1,0:T(8,128)(2,1)S(1)} %shard_map.89), channel_id=1, replica_groups=mesh['half'=2,'head'=8,'member'=2,'dp'=1] {'head'}, dimensions={0} | all-to-all | bytes 1048576 | tf_op jit(solution)/shard_map/all_to_all | solution.py:397
  48.8 1.3 %shard_map.90 = (bf16[128,1024]{1,0:T(8,128)(2,1)}, bf16[128,1024]{1,0:T(8,128)(2,1)}, bf16[128,1024]{1,0:T(8,128)(2,1)}, bf16[128,1024]{1,0:T(8,128)(2,1)}) custom-call(bf16[8,256,128]{2,1,0:T(8,128)(2,1)S(1)} %all_to_all.10.in_ref), custom_call_target="tpu_custom_call" | custom-call | tf_op jit(solution)/shard_map/pallas_call | solution.py:458
  (10 shorter events, 0.1 us)
Async XLA Ops:
  3.0 15.6 %all-to-all-start = ((bf16[8,272,128]{2,1,0:T(8,128)(2,1)}), bf16[8,272,128]{2,1,0:T(8,128)(2,1)S(1)}, u32[]{:S(2)}, u32[]{:S(2)}) async-start(bf16[8,272,128]{2,1,0:T(8,128)(2,1)} %shard_map.84), calls=%async_computation | async-start | bytes 1114112 | tf_op jit(solution)/shard_map/all_to_all | solution.py:397
  18.6 3.2 %collective-permute-start.3 = (bf16[8,208,128]{2,1,0:T(8,128)(2,1)S(1)}, bf16[8,208,128]{2,1,0:T(8,128)(2,1)S(1)}, u32[]{:S(2)}, u32[]{:S(2)}) collective-permute-start(bf16[8,208,128]{2,1,0:T(8,128)(2,1)S(1)} %slice.44), channel_id=1, source_target_pairs={{0,1},{1,0},{2,3},{3,2},{4,5},{5,4},{6,7},{7,6},{8,9},{9,8},{10,11... | collective-permute-start | bytes 1277960 | tf_op jit(solution)/shard_map/ppermute | solution.py:400
  18.8 8.8 %collective-permute-start.2 = (bf16[272,128]{1,0:T(8,128)(2,1)S(1)}, bf16[272,128]{1,0:T(8,128)(2,1)S(1)}, u32[]{:S(2)}, u32[]{:S(2)}) collective-permute-start(bf16[272,128]{1,0:T(8,128)(2,1)S(1)} %fusion.2), channel_id=1, source_target_pairs={{0,16},{16,0},{1,17},{17,1},{2,18},{18,2},{3,19},{19,3},{4,20},{20... | collective-permute-start | bytes 208904 | tf_op jit(solution)/shard_map/ppermute | solution.py:403
  21.5 7.2 %collective-permute-start = (bf16[256,128]{1,0:T(8,128)(2,1)S(1)}, bf16[256,128]{1,0:T(8,128)(2,1)S(1)}, u32[]{:S(2)}, u32[]{:S(2)}) collective-permute-start(bf16[256,128]{1,0:T(8,128)(2,1)S(1)} %pad_maximum_fusion), channel_id=1, source_target_pairs={{0,16},{16,0},{1,17},{17,1},{2,18},{18,2},{3,19},{19,3},{4,20},{20... | collective-permute-start | bytes 196616 | tf_op jit(solution)/shard_map/ppermute | solution.py:403
  27.6 1.3 %collective-permute-start.4 = (bf16[272,128]{1,0:T(8,128)(2,1)S(1)}, bf16[272,128]{1,0:T(8,128)(2,1)S(1)}, u32[]{:S(2)}, u32[]{:S(2)}) collective-permute-start(bf16[272,128]{1,0:T(8,128)(2,1)S(1)} %collective-permute-done.2.refs_0_.refs_2_), channel_id=1, source_target_pairs={{0,1},{1,0},{2,3},{3,2},{4,5},{5,4},{6,7},{7,6},{8,9},{9,8},{10,11... | collective-permute-start | bytes 208904 | tf_op jit(solution)/shard_map/ppermute | solution.py:400
  28.6 1.3 %collective-permute-start.1 = (bf16[256,128]{1,0:T(8,128)(2,1)S(1)}, bf16[256,128]{1,0:T(8,128)(2,1)S(1)}, u32[]{:S(2)}, u32[]{:S(2)}) collective-permute-start(bf16[256,128]{1,0:T(8,128)(2,1)S(1)} %collective-permute-done.refs_0_), channel_id=1, source_target_pairs={{0,1},{1,0},{2,3},{3,2},{4,5},{5,4},{6,7},{7,6},{8,9},{9,8},{10,11... | collective-permute-start | bytes 196616 | tf_op jit(solution)/shard_map/ppermute | solution.py:400
  30.4 1.2 %collective-permute-start.5 = (f32[8,128]{1,0:T(8,128)S(1)}, f32[8,128]{1,0:T(8,128)S(1)}, u32[]{:S(2)}, u32[]{:S(2)}) collective-permute-start(f32[8,128]{1,0:T(8,128)S(1)} %get-tuple-element.59), channel_id=1, source_target_pairs={{0,1},{1,0},{2,3},{3,2},{4,5},{5,4},{6,7},{7,6},{8,9},{9,8},{10,11... | collective-permute-start | bytes 12296 | tf_op jit(solution)/shard_map/ppermute | solution.py:400
  31.6 4.7 %collective-permute-start.7 = (bf16[8,192,128]{2,1,0:T(8,128)(2,1)S(1)}, bf16[8,192,128]{2,1,0:T(8,128)(2,1)S(1)}, u32[]{:S(2)}, u32[]{:S(2)}) collective-permute-start(bf16[8,192,128]{2,1,0:T(8,128)(2,1)S(1)} %get-tuple-element.67), channel_id=1, source_target_pairs={{0,1},{1,0},{2,3},{3,2},{4,5},{5,4},{6,7},{7,6},{8,9},{9,8},{10,11... | collective-permute-start | bytes 1179656 | tf_op jit(solution)/shard_map/ppermute | solution.py:400
  31.8 4.5 %collective-permute-start.6 = (f32[16,128]{1,0:T(8,128)S(1)}, f32[16,128]{1,0:T(8,128)S(1)}, u32[]{:S(2)}, u32[]{:S(2)}) collective-permute-start(f32[16,128]{1,0:T(8,128)S(1)} %pad_maximum_fusion.1), channel_id=1, source_target_pairs={{0,16},{16,0},{1,17},{17,1},{2,18},{18,2},{3,19},{19,3},{4,20},{20... | collective-permute-start | bytes 24584 | tf_op jit(solution)/shard_map/ppermute | solution.py:403

commit v6 on v4

--- a/solution.py
+++ b/solution.py
@@ -42,6 +42,10 @@
 
 def takes_fine(members):
     return lax.axis_index("member") >= members // 2
+
+
+def column_chunks():
+    return [((h, h + 1), slice(h * HD, (h + 2) * HD)) for h in range(0, H, 2)]
 
 
 def pack_kernel(r0, rows, members, q_in, k_in, v_in, g_in, doc_in, out, q_ref, k_ref, v_ref, g_ref, doc_ref, buf, sem):
@@ -352,13 +356,14 @@
     query_sels = [selector(h, r0, rows, tokens, True, takes_fine(members)) for h in kinds]
     key_sels = [selector(h, r0, rows, tokens, True, True) for h in kinds]
     copies = []
-    for i, base in enumerate((0, 1, 4, 5)):
-        for h in range(H):
+    for heads, cols in column_chunks():
+        for i, base in enumerate((0, 1, 4, 5)):
             sels = query_sels if i < 2 else key_sels
-            part = jnp.concatenate([in_ref[h, (base + e) * rows:(base + e + 1) * rows] for e in (0, 2)], 0)
-            bufs[i][:, h * HD:(h + 1) * HD] = dot_nn(sels[h % (2 * r0)], part).astype(bf16)
-        copies.append(pltpu.make_async_copy(bufs[i], outs[i], sem.at[i]))
-        copies[-1].start()
+            for h in heads:
+                part = jnp.concatenate([in_ref[h, (base + e) * rows:(base + e + 1) * rows] for e in (0, 2)], 0)
+                bufs[i][:, h * HD:(h + 1) * HD] = dot_nn(sels[h % (2 * r0)], part).astype(bf16)
+            copies.append(pltpu.make_async_copy(bufs[i].at[:, cols], outs[i].at[:, cols], sem.at[len(copies)]))
+            copies[-1].start()
     for copy in copies:
         copy.wait()
 
@@ -456,7 +461,7 @@
     back = to_head(back)
     return tuple(call(
         functools.partial(unpack_kernel, r0, rows, G), [shape((tokens, H * HD), bf16)] * 4,
-        [wide] * 4 + [pltpu.SemaphoreType.DMA((4,))],
+        [wide] * 4 + [pltpu.SemaphoreType.DMA((2 * H,))],
         in_specs=[VMEM], out_specs=[anywhere] * 4,
     )(back))
 

time: 50.3 us -> 50.3 us (level)
  no operation moved by 1% of the time
where the time goes in v6:
time: 50.3 us; the launch traced here: 50.1 us
  waiting for transfers between devices  19.6 us (39%)
  blocking collectives  12 us (24%)
  starting transfers between devices  10.3 us (20%)
  Pallas kernels  7.36 us (15%)
  between operations  0.73 us (1%)
    all_to_all x1, blocking collectives, to_head(): return lax.all_to_all(x, 'head', 0, 0, tiled=True)  12 us
    all_to_all x1, waiting for transfers between devices, to_head(): return lax.all_to_all(x, 'head', 0, 0, tiled=True)  9.42 us
    ppermute x3, waiting for transfers between devices, across(): return lax.ppermute(x, 'half', [(0, 1), (1, 0)])  8.63 us
    all_to_all x1, starting transfers between devices, to_head(): return lax.all_to_all(x, 'head', 0, 0, tiled=True)  6.2 us
    ppermute x3, starting transfers between devices, across(): return lax.ppermute(x, 'half', [(0, 1), (1, 0)])  3.66 us
    pallas_call x1, Pallas kernels, per_device(): call(functools.partial(pack_kernel, r0, rows, G), shape(message, bf16), [...  2.35 us
    pallas_call x1, Pallas kernels, per_device(): call(functools.partial(local_kernel, r0, rows, G), [shape((n, HD), bf16)]...  1.64 us
    ppermute x5, waiting for transfers between devices, to_member(): return lax.ppermute(x, 'member', [(i, i ^ g) for i in range(G)])  1.51 us
  transfers between devices with their start and end apart: 9, of which 7 were waited for; matrix products, arithmetic and copies ran while one was open for 0% of the time, Pallas kernels for 6%

profile of v6, /device:TPU:0, one launch (start us, length us, event | category | flops | bytes accessed | tf_op | source)
XLA Modules:
  0.0 50.1 jit_solution(16125279186981383279)
XLA Ops:
  0.6 2.3 %shard_map.84 = bf16[8,272,128]{2,1,0:T(8,128)(2,1)} custom-call(bf16[128,1024]{1,0:T(8,128)(2,1)} %q_in.1, bf16[128,1024]{1,0:T(8,128)(2,1)} %k_in.1, bf16[128,1024]{1,0:T(8,128)(2,1)} %v_in.1, bf16[128,1024]{1,0:T(8,128)(2,1)} %g_in.1, s32[1,128]{1,0:T(1,128)} %bitcast.13), custom_call_target="tpu_custom_call" | custom-call | tf_op jit(solution)/shard_map/pallas_call | solution.py:394
  3.0 6.2 %all-to-all-start = ((bf16[8,272,128]{2,1,0:T(8,128)(2,1)}), bf16[8,272,128]{2,1,0:T(8,128)(2,1)S(1)}, u32[]{:S(2)}, u32[]{:S(2)}) async-start(bf16[8,272,128]{2,1,0:T(8,128)(2,1)} %shard_map.84), calls=%async_computation | async-start | bytes 1114112 | tf_op jit(solution)/shard_map/all_to_all | solution.py:401
  9.2 9.4 %all-to-all-done.refs_0_.own_ref = bf16[8,272,128]{2,1,0:T(8,128)(2,1)S(1)} async-done(((bf16[8,272,128]{2,1,0:T(8,128)(2,1)}), bf16[8,272,128]{2,1,0:T(8,128)(2,1)S(1)}, u32[]{:S(2)}, u32[]{:S(2)}) %all-to-all-start) | async-done | bytes 557088 | tf_op jit(solution)/shard_map/all_to_all | solution.py:401
  18.6 0.1 collective-permute-start.3
  18.8 2.7 %collective-permute-start.2 = (bf16[272,128]{1,0:T(8,128)(2,1)S(1)}, bf16[272,128]{1,0:T(8,128)(2,1)S(1)}, u32[]{:S(2)}, u32[]{:S(2)}) collective-permute-start(bf16[272,128]{1,0:T(8,128)(2,1)S(1)} %fusion.2), channel_id=1, source_target_pairs={{0,16},{16,0},{1,17},{17,1},{2,18},{18,2},{3,19},{19,3},{4,20},{20... | collective-permute-start | bytes 208904 | tf_op jit(solution)/shard_map/ppermute | solution.py:407
  21.5 0.3 collective-permute-start
  21.8 0.0 collective-permute-done.3.refs_1_
  21.8 1.6 %shard_map.85 = (bf16[512,128]{1,0:T(8,128)(2,1)S(1)}, bf16[512,128]{1,0:T(8,128)(2,1)S(1)}, bf16[512,128]{1,0:T(8,128)(2,1)S(1)}, bf16[512,128]{1,0:T(8,128)(2,...) custom-call(bf16[8,272,128]{2,1,0:T(8,128)(2,1)S(1)} %all-to-all-don, ...), custom_call_target="tpu_custom_call" | custom-call | tf_op jit(solution)/shard_map/pallas_call | solution.py:425
  23.5 4.2 %collective-permute-done.2.refs_0_.refs_2_ = bf16[272,128]{1,0:T(8,128)(2,1)S(1)} collective-permute-done((bf16[272,128]{1,0:T(8,128)(2,1)S(1)}, bf16[272,128]{1,0:T(8,128)(2,1)S(1)}, u32[]{:S(2)}, u32[]{:S(2)}) %collective-permute-start.2) | collective-permute-done | bytes 69664 | tf_op jit(solution)/shard_map/ppermute | solution.py:407
  27.6 1.0 %collective-permute-done.refs_0_ = bf16[256,128]{1,0:T(8,128)(2,1)S(1)} collective-permute-done((bf16[256,128]{1,0:T(8,128)(2,1)S(1)}, bf16[256,128]{1,0:T(8,128)(2,1)S(1)}, u32[]{:S(2)}, u32[]{:S(2)}) %collective-permute-start) | collective-permute-done | bytes 65568 | tf_op jit(solution)/shard_map/ppermute | solution.py:407
  28.6 0.3 collective-permute-done.4.refs_1_.refs_3_
  28.9 0.7 %shard_map.86 = (f32[8,128]{1,0:T(8,128)S(1)}, bf16[256,128]{1,0:T(8,128)(2,1)S(1)}, bf16[256,128]{1,0:T(8,128)(2,1)S(1)}, f32[512,128]{1,0:T(8,128)S(1)}, f32[5...) custom-call(bf16[272,128]{1,0:T(8,128)(2,1)S(1)} %collective-permute-done.2.refs_0_.refs_2_, ...), custom_call_target="tpu_custom_call" | custom-call | tf_op jit(solution)/shard_map/pallas_call | solution.py:435
  29.7 0.2 collective-permute-done.1.refs_1_
  29.9 0.6 %shard_map.87 = (f32[8,128]{1,0:T(8,128)S(1)}, bf16[8,64,128]{2,1,0:T(8,128)(2,1)S(1)}, f32[8,128,128]{2,1,0:T(8,128)S(1)}, bf16[8,192,128]{2,1,0:T(8,128)(2,1)S(1)}) custom-call(bf16[256,128]{1,0:T(8,128)(2,1)S(1)} %collective-permute-done.refs_0_, bf16[256,128]{1,0:T(8,128)(2,1)S(1)} %collective-permute-done.1.refs_1_, ...), custom_call_target="tpu_custom_call" | custom-call | tf_op jit(solution)/shard_map/pallas_call | solution.py:442
  30.5 0.2 collective-permute-start.5
  30.7 1.0 %collective-permute-done.5 = f32[8,128]{1,0:T(8,128)S(1)} collective-permute-done((f32[8,128]{1,0:T(8,128)S(1)}, f32[8,128]{1,0:T(8,128)S(1)}, u32[]{:S(2)}, u32[]{:S(2)}) %collective-permute-start.5) | collective-permute-done | bytes 4128 | tf_op jit(solution)/shard_map/ppermute | solution.py:404
  31.7 0.2 collective-permute-start.7
  31.9 0.7 %collective-permute-start.6 = (f32[16,128]{1,0:T(8,128)S(1)}, f32[16,128]{1,0:T(8,128)S(1)}, u32[]{:S(2)}, u32[]{:S(2)}) collective-permute-start(f32[16,128]{1,0:T(8,128)S(1)} %pad_maximum_fusion.1), channel_id=1, source_target_pairs={{0,16},{16,0},{1,17},{17,1},{2,18},{18,2},{3,19},{19,3},{4,20},{20... | collective-permute-start | bytes 24584 | tf_op jit(solution)/shard_map/ppermute | solution.py:407
  32.6 0.4 shard_map.88
  33.0 3.4 %collective-permute-done.6.refs_4_ = f32[16,128]{1,0:T(8,128)S(1)} collective-permute-done((f32[16,128]{1,0:T(8,128)S(1)}, f32[16,128]{1,0:T(8,128)S(1)}, u32[]{:S(2)}, u32[]{:S(2)}) %collective-permute-start.6) | collective-permute-done | bytes 8224 | tf_op jit(solution)/shard_map/ppermute | solution.py:407
  36.4 0.0 collective-permute-done.7.refs_11_
  36.4 0.4 shard_map.89
  36.8 12.0 %all_to_all.10.in_ref = bf16[8,256,128]{2,1,0:T(8,128)(2,1)S(1)} all-to-all(bf16[8,256,128]{2,1,0:T(8,128)(2,1)S(1)} %shard_map.89), channel_id=1, replica_groups=mesh['half'=2,'head'=8,'member'=2,'dp'=1] {'head'}, dimensions={0} | all-to-all | bytes 1048576 | tf_op jit(solution)/shard_map/all_to_all | solution.py:401
  48.8 1.3 %shard_map.90 = (bf16[128,1024]{1,0:T(8,128)(2,1)}, bf16[128,1024]{1,0:T(8,128)(2,1)}, bf16[128,1024]{1,0:T(8,128)(2,1)}, bf16[128,1024]{1,0:T(8,128)(2,1)}) custom-call(bf16[8,256,128]{2,1,0:T(8,128)(2,1)S(1)} %all_to_all.10.in_ref), custom_call_target="tpu_custom_call" | custom-call | tf_op jit(solution)/shard_map/pallas_call | solution.py:462
  (10 shorter events, 0.1 us)
Async XLA Ops:
  3.0 15.6 %all-to-all-start = ((bf16[8,272,128]{2,1,0:T(8,128)(2,1)}), bf16[8,272,128]{2,1,0:T(8,128)(2,1)S(1)}, u32[]{:S(2)}, u32[]{:S(2)}) async-start(bf16[8,272,128]{2,1,0:T(8,128)(2,1)} %shard_map.84), calls=%async_computation | async-start | bytes 1114112 | tf_op jit(solution)/shard_map/all_to_all | solution.py:401
  18.6 3.2 %collective-permute-start.3 = (bf16[8,208,128]{2,1,0:T(8,128)(2,1)S(1)}, bf16[8,208,128]{2,1,0:T(8,128)(2,1)S(1)}, u32[]{:S(2)}, u32[]{:S(2)}) collective-permute-start(bf16[8,208,128]{2,1,0:T(8,128)(2,1)S(1)} %slice.44), channel_id=1, source_target_pairs={{0,1},{1,0},{2,3},{3,2},{4,5},{5,4},{6,7},{7,6},{8,9},{9,8},{10,11... | collective-permute-start | bytes 1277960 | tf_op jit(solution)/shard_map/ppermute | solution.py:404
  18.8 8.8 %collective-permute-start.2 = (bf16[272,128]{1,0:T(8,128)(2,1)S(1)}, bf16[272,128]{1,0:T(8,128)(2,1)S(1)}, u32[]{:S(2)}, u32[]{:S(2)}) collective-permute-start(bf16[272,128]{1,0:T(8,128)(2,1)S(1)} %fusion.2), channel_id=1, source_target_pairs={{0,16},{16,0},{1,17},{17,1},{2,18},{18,2},{3,19},{19,3},{4,20},{20... | collective-permute-start | bytes 208904 | tf_op jit(solution)/shard_map/ppermute | solution.py:407
  21.5 7.2 %collective-permute-start = (bf16[256,128]{1,0:T(8,128)(2,1)S(1)}, bf16[256,128]{1,0:T(8,128)(2,1)S(1)}, u32[]{:S(2)}, u32[]{:S(2)}) collective-permute-start(bf16[256,128]{1,0:T(8,128)(2,1)S(1)} %pad_maximum_fusion), channel_id=1, source_target_pairs={{0,16},{16,0},{1,17},{17,1},{2,18},{18,2},{3,19},{19,3},{4,20},{20... | collective-permute-start | bytes 196616 | tf_op jit(solution)/shard_map/ppermute | solution.py:407
  27.6 1.3 %collective-permute-start.4 = (bf16[272,128]{1,0:T(8,128)(2,1)S(1)}, bf16[272,128]{1,0:T(8,128)(2,1)S(1)}, u32[]{:S(2)}, u32[]{:S(2)}) collective-permute-start(bf16[272,128]{1,0:T(8,128)(2,1)S(1)} %collective-permute-done.2.refs_0_.refs_2_), channel_id=1, source_target_pairs={{0,1},{1,0},{2,3},{3,2},{4,5},{5,4},{6,7},{7,6},{8,9},{9,8},{10,11... | collective-permute-start | bytes 208904 | tf_op jit(solution)/shard_map/ppermute | solution.py:404
  28.6 1.3 %collective-permute-start.1 = (bf16[256,128]{1,0:T(8,128)(2,1)S(1)}, bf16[256,128]{1,0:T(8,128)(2,1)S(1)}, u32[]{:S(2)}, u32[]{:S(2)}) collective-permute-start(bf16[256,128]{1,0:T(8,128)(2,1)S(1)} %collective-permute-done.refs_0_), channel_id=1, source_target_pairs={{0,1},{1,0},{2,3},{3,2},{4,5},{5,4},{6,7},{7,6},{8,9},{9,8},{10,11... | collective-permute-start | bytes 196616 | tf_op jit(solution)/shard_map/ppermute | solution.py:404
  30.5 1.2 %collective-permute-start.5 = (f32[8,128]{1,0:T(8,128)S(1)}, f32[8,128]{1,0:T(8,128)S(1)}, u32[]{:S(2)}, u32[]{:S(2)}) collective-permute-start(f32[8,128]{1,0:T(8,128)S(1)} %get-tuple-element.59), channel_id=1, source_target_pairs={{0,1},{1,0},{2,3},{3,2},{4,5},{5,4},{6,7},{7,6},{8,9},{9,8},{10,11... | collective-permute-start | bytes 12296 | tf_op jit(solution)/shard_map/ppermute | solution.py:404
  31.7 4.7 %collective-permute-start.7 = (bf16[8,192,128]{2,1,0:T(8,128)(2,1)S(1)}, bf16[8,192,128]{2,1,0:T(8,128)(2,1)S(1)}, u32[]{:S(2)}, u32[]{:S(2)}) collective-permute-start(bf16[8,192,128]{2,1,0:T(8,128)(2,1)S(1)} %get-tuple-element.67), channel_id=1, source_target_pairs={{0,1},{1,0},{2,3},{3,2},{4,5},{5,4},{6,7},{7,6},{8,9},{9,8},{10,11... | collective-permute-start | bytes 1179656 | tf_op jit(solution)/shard_map/ppermute | solution.py:404
  31.9 4.5 %collective-permute-start.6 = (f32[16,128]{1,0:T(8,128)S(1)}, f32[16,128]{1,0:T(8,128)S(1)}, u32[]{:S(2)}, u32[]{:S(2)}) collective-permute-start(f32[16,128]{1,0:T(8,128)S(1)} %pad_maximum_fusion.1), channel_id=1, source_target_pairs={{0,16},{16,0},{1,17},{17,1},{2,18},{18,2},{3,19},{19,3},{4,20},{20... | collective-permute-start | bytes 24584 | tf_op jit(solution)/shard_map/ppermute | solution.py:407
